TPU v7x, 32 devices: a whole 2x2x4 slice. The times are simulated.
32 devices in a mesh: dp: 8 (over y, x, core), mp: 4 (over z).
Axes of the slice: x: 2, y: 2, z: 4, core: 2. Of those that a mesh axis runs over, the one named last changes fastest.
Arguments:
- response_query: bfloat16 [384, 8, 6144], P('dp', None, 'mp'), may hold values from -80 to 80, as said below
- response_keys: bfloat16 [2, 384, 8, 768], P(None, 'dp'), may hold values from -8 to 8
- prompt_cache: bfloat16 [2, 8, 1024, 768], P(None, 'dp'), may hold values from -6 to 6
- lengths: int32 [384], P('dp'), may hold values from 1 to 8, as said below
- owners: int32 [384], P('dp'), may hold values from 0 to 7, as said below
- pairing: int32 [384], replicated, may hold values from 0 to 383, each once
- residual: bfloat16 [384, 8192], P(None, 'dp'), may hold values from -90 to 90
- output_weight: bfloat16 [6144, 8192], P('mp', 'dp'), may hold values from -0.3125 to 0.3125
- norm_gain: float32 [8192], P('dp'), may hold values from 0.1 to 1.9
- reward_head: float32 [8192], P('dp'), may hold values from -0.0625 to 0.0625
Outputs:
- attention_rows: bfloat16 [384, 8, 6144], P('dp', None, 'mp')
- rewards: float32 [384], replicated
- pair_loss: float32 [], replicated
- weight_gradient: float32 [6144, 8192], P('mp', 'dp')
- head_gradient: float32 [8192], P('dp')
- pooled_gradient: float32 [384, 6144], P('dp', 'mp')
Inputs may be any that keep to these rules, and one draw needn't show every extreme that they name: `response_query`: drawn jointly with response_keys. `lengths`: every dp index holds a response of length 8. The responses of one dp index spread over owners as evenly as possible: each owner receives at most 6 of them, and some owner receives exactly 6.
All inputs are finite; a program needn't handle non-finite values.
Results may differ from a plain program's by a relative error of at most 0.0056.
Values may be sent and summed in bfloat16 or wider, within the bound.
A program may use at most 64 MiB of HBM per device.

v0:
```python
import functools
import math

import jax
import jax.numpy as jnp
from jax import lax
from jax.experimental import pallas as pl
from jax.experimental.pallas import tpu as pltpu
from jax.sharding import PartitionSpec as P

D = 8192
HD = 128
Q_HEADS = 48
KV_HEADS = 6


EPSILON = 1e-05


def bradley_terry(rewards, pairing):
    count = rewards.shape[0]
    chosen = pairing[0::2, None] == jnp.arange(count)[None, :]
    rejected = pairing[1::2, None] == jnp.arange(count)[None, :]
    sign = chosen.astype(jnp.float32) - rejected.astype(jnp.float32)
    margin = jnp.sum(sign * rewards[None, :], axis=1)
    loss_value = jnp.mean(jax.nn.softplus(-margin))
    slope = -jax.nn.sigmoid(-margin) / margin.shape[0]
    reward_slope = jnp.sum(sign * slope[:, None], axis=0)
    return (loss_value, reward_slope)


def pack_kernel(window, meta, query, keys, out, late):
    slots = out.shape[0]
    rest = late.shape[2]
    width = query.shape[2] - rest
    span = window * HD
    first = pl.multiple_of(meta[2 * slots] * HD, HD)

    def body(p, carry):
        r = meta[p]
        out[p, :, pl.ds(0, width)] = query[r, :, pl.ds(0, width)]
        late[p] = query[r, :, pl.ds(width, rest)]
        out[p, :, pl.ds(width, span)] = keys[0, r, :, pl.ds(first, span)]
        out[p, :, pl.ds(width + span, span)] = keys[1, r, :, pl.ds(first, span)]
        length = meta[slots + p].astype(jnp.float32)
        place = r.astype(jnp.float32)
        lane = lax.broadcasted_iota(jnp.int32, (out.shape[1], HD), 1)
        out[p, :, pl.ds(width + 2 * span, HD)] = jnp.where(lane < HD // 2, length, place).astype(
            jnp.bfloat16
        )
        return carry

    lax.fori_loop(0, slots, body, 0)


def attention_kernel(slot_count, placed, meta, query, own_k, own_v, lens, cache, out, pooled):
    rows = query.shape[0]
    head = pl.program_id(0)
    chunk = 128
    blocks = chunk // slot_count
    scale = math.log2(math.e) / math.sqrt(HD)
    contract = (((1,), (1,)), ((), ()))
    row = lax.broadcasted_iota(jnp.int32, (chunk, chunk), 0)
    col = lax.broadcasted_iota(jnp.int32, (chunk, chunk), 1)
    t = row % slot_count
    s = col % slot_count
    causal = (row // slot_count == col // slot_count) & (s <= t)
    s_float = s.astype(jnp.float32)
    t_float = t.astype(jnp.float32)
    gather = lax.broadcasted_iota(jnp.int32, (blocks, chunk), 0)
    member = lax.broadcasted_iota(jnp.int32, (blocks, chunk), 1)
    gather = jnp.where(gather == member // slot_count, 1.0, 0.0).astype(jnp.bfloat16)
    for start in range(0, rows, chunk):
        here = pl.ds(start, chunk)
        q = query[here, :]
        length = jnp.broadcast_to(lens[here, :].astype(jnp.float32)[:, 0:1], (chunk, chunk))
        far = lax.dot_general(q, cache[0, 0], contract, preferred_element_type=jnp.float32)
        near = lax.dot_general(q, own_k[here, :], contract, preferred_element_type=jnp.float32)
        near = jnp.where(causal & (s_float < length), near, -jnp.inf)
        top = jnp.maximum(
            jnp.max(far, axis=1, keepdims=True), jnp.max(near, axis=1, keepdims=True)
        )
        far = jnp.exp2((far - top) * scale)
        near = jnp.exp2((near - top) * scale)
        total = jnp.sum(far, axis=1, keepdims=True) + jnp.sum(near, axis=1, keepdims=True)
        value = jnp.dot(far.astype(jnp.bfloat16), cache[1, 0], preferred_element_type=jnp.float32)
        value += jnp.dot(
            near.astype(jnp.bfloat16), own_v[here, :], preferred_element_type=jnp.float32
        )
        value = jnp.where(t_float < length, value / total, 0.0)
        out[here, :] = value.astype(jnp.bfloat16)
        last = jnp.where(t_float == length - 1.0, value, 0.0)
        last = jnp.dot(gather, last.astype(jnp.bfloat16), preferred_element_type=jnp.float32)
        there = pl.ds(start // slot_count, blocks)
        pooled[there, pl.ds(pl.multiple_of(head * HD, HD), HD)] = last.astype(jnp.bfloat16)

        if placed:

            @pl.when(head == 0)
            def _():
                place = lens[here, :].astype(jnp.float32).reshape(blocks, slot_count, HD)
                pooled[there, pl.ds(pooled.shape[1] - HD, HD)] = jnp.max(place, axis=1).astype(
                    jnp.bfloat16
                )


def unpack_kernel(meta, returned, out):
    def body(r, carry):
        out[r] = returned[meta[r]]
        return carry

    lax.fori_loop(0, out.shape[0], body, 0)


def shards(
    response_query,
    response_keys,
    prompt_cache,
    lengths,
    owners,
    pairing,
    residual,
    output_weight,
    norm_gain,
    reward_head,
):
    groups = lax.axis_size("dp")
    planes = lax.axis_size("mp")
    model_rank = lax.axis_index("mp")
    held_count, slot_count, head_width = response_query.shape
    local_heads = head_width // HD
    group_size = Q_HEADS // KV_HEADS
    per_owner = (held_count + groups - 1) // groups
    capacity = groups * per_owner
    window = max(
        (m * local_heads + local_heads - 1) // group_size - m * local_heads // group_size + 1
        for m in range(planes)
    )
    first_head = jnp.minimum(model_rank * local_heads // group_size, KV_HEADS - window)
    head_kv = (model_rank * local_heads + jnp.arange(local_heads)) // group_size
    positions = jnp.arange(held_count)
    earlier = (owners[None, :] == owners[:, None]) & (positions[None, :] < positions[:, None])
    target = (owners * per_owner + jnp.sum(earlier, axis=1)).astype(jnp.int32)
    sent_from = (target[None, :] == jnp.arange(capacity)[:, None]).astype(jnp.int32)
    source = jnp.sum(sent_from * positions[None, :], axis=1)
    slot_length = jnp.sum(sent_from * lengths[None, :], axis=1)
    params = pltpu.CompilerParams(vmem_limit_bytes=40 * 1024 * 1024)
    vmem = pl.BlockSpec(memory_space=pltpu.VMEM)
    smem = pl.BlockSpec(memory_space=pltpu.SMEM)
    early = local_heads - local_heads // 2
    late_width = local_heads // 2 * HD
    packed_width = early * HD + (2 * window + 1) * HD
    packed, late = pl.pallas_call(
        functools.partial(pack_kernel, window),
        out_shape=(
            jax.ShapeDtypeStruct((capacity, slot_count, packed_width), jnp.bfloat16),
            jax.ShapeDtypeStruct((capacity, slot_count, late_width), jnp.bfloat16),
        ),
        in_specs=[smem, vmem, vmem],
        out_specs=(vmem, vmem),
        compiler_params=params,
        name="pack",
    )(
        jnp.concatenate([source, slot_length, first_head[None]]).astype(jnp.int32),
        response_query,
        response_keys,
    )
    packed = packed.reshape(groups, per_owner, slot_count, packed_width)
    arrived = lax.all_to_all(packed, "dp", split_axis=0, concat_axis=0, tiled=True)
    late = late.reshape(groups, per_owner, slot_count, late_width)
    late = lax.all_to_all(late, "dp", split_axis=0, concat_axis=0, tiled=True)
    rows = capacity * slot_count
    late = late.reshape(rows, late_width)
    arrived = arrived.reshape(rows, packed_width)
    block = (rows, HD)

    def attend(query, head_base, heads, placed):
        pooled_width = (heads + placed) * HD
        at = lambda meta, h: meta[local_heads + head_base + h]
        return pl.pallas_call(
            functools.partial(attention_kernel, slot_count, placed),
            out_shape=(
                jax.ShapeDtypeStruct((rows, heads * HD), jnp.bfloat16),
                jax.ShapeDtypeStruct((capacity, pooled_width), jnp.bfloat16),
            ),
            grid_spec=pltpu.PrefetchScalarGridSpec(
                num_scalar_prefetch=1,
                grid=(heads,),
                in_specs=[
                    pl.BlockSpec(block, lambda h, meta: (0, h)),
                    pl.BlockSpec(block, lambda h, meta: (0, early + at(meta, h))),
                    pl.BlockSpec(block, lambda h, meta: (0, early + window + at(meta, h))),
                    pl.BlockSpec(block, lambda h, meta: (0, early + 2 * window)),
                    pl.BlockSpec(
                        (2, 1, prompt_cache.shape[2], HD),
                        lambda h, meta: (0, 0, 0, meta[head_base + h]),
                    ),
                ],
                out_specs=(
                    pl.BlockSpec(block, lambda h, meta: (0, h)),
                    pl.BlockSpec((capacity, pooled_width), lambda h, meta: (0, 0)),
                ),
            ),
            compiler_params=params,
            cost_estimate=pl.CostEstimate(
                flops=4 * rows * heads * HD * prompt_cache.shape[2],
                bytes_accessed=8 * rows * heads * HD,
                transcendentals=rows * heads * prompt_cache.shape[2],
            ),
            name="attention_early" if placed else "attention_late",
        )(
            jnp.concatenate([head_kv, head_kv - first_head]).astype(jnp.int32),
            query,
            arrived,
            arrived,
            arrived,
            prompt_cache,
        )

    def share_rows(own):
        copies = jnp.broadcast_to(own[None], (groups,) + own.shape)
        copies = lax.all_to_all(copies, "dp", split_axis=0, concat_axis=0, tiled=True)
        return copies.reshape(groups * own.shape[0], own.shape[1])

    attended_early, pooled_early = attend(arrived, 0, early, True)
    pooled_slots = share_rows(pooled_early)
    attended_late, pooled_late = attend(late, early, local_heads - early, False)
    pooled_late = share_rows(pooled_late)
    attended = jnp.concatenate([attended_early, attended_late], axis=1)
    result = attended.reshape(groups, per_owner, slot_count, head_width)
    returned = lax.all_to_all(result, "dp", split_axis=0, concat_axis=0, tiled=True)
    attention_rows = pl.pallas_call(
        unpack_kernel,
        out_shape=jax.ShapeDtypeStruct(response_query.shape, jnp.bfloat16),
        in_specs=[smem, vmem],
        out_specs=vmem,
        compiler_params=params,
        name="unpack",
    )(target, returned.reshape(capacity, slot_count, head_width))
    count = held_count * groups
    sender = jnp.arange(capacity * groups) % capacity // per_owner
    place = pooled_slots[:, early * HD + HD - 1].astype(jnp.int32)
    live = pooled_slots[:, early * HD] > 0
    response = jnp.where(live, sender * held_count + place, count)
    order = (jnp.arange(count)[:, None] == response[None, :]).astype(jnp.bfloat16)
    pooled_all = jnp.concatenate(
        [
            jnp.dot(order, slots, preferred_element_type=jnp.float32).astype(jnp.bfloat16)
            for slots in (pooled_slots[:, : early * HD], pooled_late)
        ],
        axis=1,
    )
    share = count // planes
    partial_mix = jnp.dot(pooled_all, output_weight, preferred_element_type=jnp.float32)
    columns = output_weight.shape[1]
    scaled_head = norm_gain * reward_head
    shares = lax.all_to_all(
        partial_mix.astype(jnp.bfloat16).reshape(planes, share, columns),
        "mp",
        split_axis=0,
        concat_axis=0,
        tiled=True,
    )
    part = jnp.sum(shares.astype(jnp.float32), axis=0) + lax.dynamic_slice_in_dim(
        residual, model_rank * share, share, 0
    ).astype(jnp.float32)
    combined = lax.all_gather(part.astype(jnp.bfloat16), "mp", axis=0, tiled=True).astype(
        jnp.float32
    )
    square_sum = jnp.sum(combined * combined, axis=1)
    signal = jnp.sum(combined * scaled_head[None, :], axis=1)
    square_sum, signal = lax.psum((square_sum, signal), "dp")
    inverse = lax.rsqrt(square_sum / D + EPSILON)
    rewards = inverse * signal
    pair_loss, reward_slope = bradley_terry(rewards, pairing)
    direct_term = reward_slope * inverse
    norm_term = reward_slope * inverse * inverse * inverse * signal / D
    upstream = direct_term[:, None] * scaled_head[None, :] - norm_term[:, None] * combined
    head_gradient = jnp.sum(direct_term[:, None] * combined * norm_gain[None, :], axis=0)
    upstream_half = upstream.astype(jnp.bfloat16)
    slope_part = lax.dot_general(
        upstream_half,
        output_weight,
        (((1,), (1,)), ((), ())),
        preferred_element_type=jnp.float32,
    ).astype(jnp.bfloat16)
    slope_parts = lax.all_to_all(
        slope_part.reshape(groups, held_count, head_width),
        "dp",
        split_axis=0,
        concat_axis=0,
        tiled=True,
    )
    weight_gradient = lax.dot_general(
        pooled_all, upstream_half, (((0,), (0,)), ((), ())), preferred_element_type=jnp.float32
    )
    pooled_gradient = jnp.sum(slope_parts.astype(jnp.float32), axis=0)
    return (attention_rows, rewards, pair_loss, weight_gradient, head_gradient, pooled_gradient)


def solution(mesh):
    placed = (
        P("dp", None, "mp"),
        P(None, "dp", None, None),
        P(None, "dp", None, None),
        P("dp"),
        P("dp"),
        P(),
        P(None, "dp"),
        P("mp", "dp"),
        P("dp"),
        P("dp"),
    )
    return jax.shard_map(
        shards,
        mesh=mesh,
        in_specs=placed,
        out_specs=(P("dp", None, "mp"), P(), P(), P("mp", "dp"), P("dp"), P("dp", "mp")),
        check_vma=False,
    )
```

profile of v0, /device:TPU:0, one launch (start us, length us, event | category | flops | bytes accessed | tf_op | source)
XLA Modules:
  0.0 182.2 jit_solution(18125250935272773442)
XLA Ops:
  6.7 20.8 %all_to_all.35 = bf16[8,6,8,1408]{3,2,1,0:T(8,128)(2,1)} all-to-all(bf16[8,6,8,1408]{3,2,1,0:T(8,128)(2,1)S(1)} %bitcast.21), channel_id=1, replica_groups=mesh['dp'=8,'mp'=4] {'dp'}, dimensions={0} | all-to-all | bytes 2162688 | tf_op jit(solution)/shard_map/all_to_all | solution.py:169
  27.5 4.2 %all-to-all-start.1 = ((bf16[8,6,8,768]{3,2,1,0:T(8,128)(2,1)}), bf16[8,6,8,768]{3,2,1,0:T(8,128)(2,1)}, u32[]{:S(2)}, u32[]{:S(2)}) async-start(bf16[8,6,8,768]{3,2,1,0:T(8,128)(2,1)} %bitcast.22), calls=%async_computation.1 | async-start | bytes 1179648 | tf_op jit(solution)/shard_map/all_to_all | solution.py:171
  33.0 1.9 %copy-done.3 = bf16[2,1,1024,768]{3,2,1,0:T(8,128)(2,1)S(1)} copy-done((bf16[2,1,1024,768]{3,2,1,0:T(8,128)(2,1)S(1)}, bf16[2,1,1024,768]{3,2,1,0:T(8,128)(2,1)}, u32[]{:S(2)}) %copy-start.3) | copy-done | bytes 3145752
  34.9 13.7 %attention_early.1 = (bf16[384,768]{1,0:T(8,128)(2,1)S(1)}, bf16[48,896]{1,0:T(8,128)(2,1)S(1)}) custom-call(s32[24]{0:T(128)S(1)} %pad_add_fusion.meta, bf16[384,1408]{1,0:T(8,128)(2,1)S(1)} %bitcast.14, bf16[384,1408]{1,0:T(8,128)(2,1)S(1)} %bitcast.15, bf16[384,1408]{1,0:T(8,128)(2,1)S(1)} %bitcast.16, bf16[384,1408]{1,0:T(8,128)(2,1)S(1)} %bitcast.17, ...), custom_call_target="tpu_custom_call" | custom-call | flops 1207959552 | bytes 2359296 | tf_op jit(solution)/shard_map/attention_early/pallas_call | solution.py:180
  50.4 4.2 %all-to-all-start.3 = ((bf16[8,48,896]{2,1,0:T(8,128)(2,1)}), bf16[8,48,896]{2,1,0:T(8,128)(2,1)}, u32[]{:S(2)}, u32[]{:S(2)}) async-start(bf16[8,48,896]{2,1,0:T(8,128)(2,1)} %broadcast_in_dim.10), calls=%async_computation.3 | async-start | bytes 1376256 | tf_op jit(solution)/shard_map/all_to_all | solution.py:222
  55.8 1.9 %copy-done.4 = bf16[2,1,1024,768]{3,2,1,0:T(8,128)(2,1)S(1)} copy-done((bf16[2,1,1024,768]{3,2,1,0:T(8,128)(2,1)S(1)}, bf16[2,1,1024,768]{3,2,1,0:T(8,128)(2,1)}, u32[]{:S(2)}) %copy-start.4) | copy-done | bytes 3145752
  57.7 12.4 %attention_late.1 = (bf16[384,768]{1,0:T(8,128)(2,1)S(1)}, bf16[48,768]{1,0:T(8,128)(2,1)S(1)}) custom-call(s32[24]{0:T(128)S(1)} %pad_add_fusion.meta, bf16[384,768]{1,0:T(8,128)(2,1)} %bitcast.4.query, bf16[384,1408]{1,0:T(8,128)(2,1)S(1)} %bitcast.18, bf16[384,1408]{1,0:T(8,128)(2,1)S(1)} %bitcast.19, bf16[384,1408]{1,0:T(8,128)(2,1)S(1)} %bitcast.20, ...), custom_call_target="tpu_custom_call" | custom-call | flops 1207959552 | bytes 2359296 | tf_op jit(solution)/shard_map/attention_late/pallas_call | solution.py:180
  71.8 4.2 %all-to-all-start.4 = ((bf16[8,48,768]{2,1,0:T(8,128)(2,1)}), bf16[8,48,768]{2,1,0:T(8,128)(2,1)}, u32[]{:S(2)}, u32[]{:S(2)}) async-start(bf16[8,48,768]{2,1,0:T(8,128)(2,1)} %broadcast_in_dim.12), calls=%async_computation.4 | async-start | bytes 1179648 | tf_op jit(solution)/shard_map/all_to_all | solution.py:222
  78.1 2.3 %convolution_convert_fusion.3 = bf16[384,768]{1,0:T(8,128)(2,1)} fusion(bf16[384,896]{1,0:T(8,128)(2,1)} %bitcast.7, s32[384]{0:T(512)S(1)} %add_select_fusion.2), kind=kOutput, calls=%fused_computation.15 | convolution fusion | flops 226934784 | bytes 1181184 | tf_op jit(solution)/shard_map/dot_general | solution.py:248
  80.5 5.9 %all-to-all-done.4 = bf16[8,48,768]{2,1,0:T(8,128)(2,1)} async-done(((bf16[8,48,768]{2,1,0:T(8,128)(2,1)}), bf16[8,48,768]{2,1,0:T(8,128)(2,1)}, u32[]{:S(2)}, u32[]{:S(2)}) %all-to-all-start.4) | async-done | bytes 589856 | tf_op jit(solution)/shard_map/all_to_all | solution.py:222
  88.0 3.5 %convolution_convert_fusion.1 = bf16[384,1024]{1,0:T(8,128)(2,1)} fusion(bf16[1536,1024]{1,0:T(8,128)(2,1)S(1)} %copy-done, bf16[384,768]{1,0:T(8,128)(2,1)S(1)} %convolution_convert_fusion.2, bf16[384,768]{1,0:T(8,128)(2,1)} %convolution_convert_fusion.3), kind=kOutput, calls=%fused_computation.13 | convolution fusion | flops 1210712064 | bytes 5111808 | tf_op jit(solution)/shard_map/dot_general | solution.py:254
  91.5 5.0 %all-to-all-start.5 = ((bf16[4,96,1024]{2,1,0:T(8,128)(2,1)}), bf16[4,96,1024]{2,1,0:T(8,128)(2,1)}, u32[]{:S(2)}, u32[]{:S(2)}) async-start(bf16[4,96,1024]{2,1,0:T(8,128)(2,1)} %bitcast.25), calls=%async_computation.5 | async-start | bytes 1572864 | tf_op jit(solution)/shard_map/all_to_all | solution.py:257
  97.0 2.3 %pad_maximum_fusion = bf16[384,1536]{1,0:T(8,128)(2,1)} fusion(bf16[384,768]{1,0:T(8,128)(2,1)} %copy-done.9, bf16[384,768]{1,0:T(8,128)(2,1)} %copy-done.8), kind=kLoop, calls=%fused_computation.16 | loop fusion | flops 2359296 | bytes 2359296 | tf_op jit(solution)/shard_map/concatenate | solution.py:229
  99.3 14.7 %all-to-all-done.5 = bf16[4,96,1024]{2,1,0:T(8,128)(2,1)} async-done(((bf16[4,96,1024]{2,1,0:T(8,128)(2,1)}), bf16[4,96,1024]{2,1,0:T(8,128)(2,1)}, u32[]{:S(2)}, u32[]{:S(2)}) %all-to-all-start.5) | async-done | bytes 786464 | tf_op jit(solution)/shard_map/all_to_all | solution.py:257
  114.0 4.8 %all-to-all-start.2 = ((bf16[8,6,8,1536]{3,2,1,0:T(8,128)(2,1)}), bf16[8,6,8,1536]{3,2,1,0:T(8,128)(2,1)}, u32[]{:S(2)}, u32[]{:S(2)}) async-start(bf16[8,6,8,1536]{3,2,1,0:T(8,128)(2,1)} %bitcast.23), calls=%async_computation.2 | async-start | bytes 2359296 | tf_op jit(solution)/shard_map/all_to_all | solution.py:231
  121.1 17.9 %all_gather.3 = bf16[384,1024]{1,0:T(8,128)(2,1)S(1)} all-gather(bf16[96,1024]{1,0:T(8,128)(2,1)S(1)} %add_convert_fusion), channel_id=1, replica_groups=mesh['dp'=8,'mp'=4] {'mp'}, dimensions={0}, use_global_device_ids=true | all-gather | bytes 983040 | tf_op jit(solution)/shard_map/all_gather | solution.py:267
  140.3 12.7 %all-reduce = (f32[384]{0:T(512)S(1)}, f32[384]{0:T(512)S(1)}) all-reduce(f32[384]{0:T(512)S(1)} %get-tuple-element.19, f32[384]{0:T(512)S(1)} %get-tuple-element.18), channel_id=1, replica_groups=mesh['dp'=8,'mp'=4] {'dp'}, use_global_device_ids=true, to_apply=%region_7.8 | all-reduce | flops 768 | bytes 6144 | tf_op jit(solution)/shard_map/psum | solution.py:272
  154.0 3.8 %convolution_convert_fusion = bf16[384,1536]{1,0:T(8,128)(2,1)} fusion(bf16[1536,1024]{1,0:T(8,128)(2,1)S(1)} %copy-done, bf16[384,1024]{1,0:T(8,128)(2,1)} %copy-done.10, f32[384]{0:T(512)S(1)} %get-tuple-element.25, f32[384]{0:T(512)S(1)} %get-tuple-element.24, f32[1024]{0:T(1024)S(1)} %mul.123), kind=kOutput, calls=%fused_computation | convolution fusion | flops 1210515456 | bytes 5118976 | tf_op jit(solution)/shard_map/dot_general | solution.py:281
  157.8 4.3 %all-to-all-start.6 = ((bf16[8,48,1536]{2,1,0:T(8,128)(2,1)}), bf16[8,48,1536]{2,1,0:T(8,128)(2,1)}, u32[]{:S(2)}, u32[]{:S(2)}) async-start(bf16[8,48,1536]{2,1,0:T(8,128)(2,1)} %bitcast.24), calls=%async_computation.6 | async-start | bytes 2359296 | tf_op jit(solution)/shard_map/all_to_all | solution.py:287
  162.0 2.6 %unpack.1 = bf16[48,8,1536]{2,1,0:T(8,128)(2,1)} custom-call(s32[48]{0:T(128)S(1)} %multiply_add_fusion.meta, bf16[48,8,1536]{2,1,0:T(8,128)(2,1)} %bitcast.6.returned), custom_call_target="tpu_custom_call" | custom-call | tf_op jit(solution)/shard_map/unpack/pallas_call | solution.py:232
  165.3 2.0 %fusion.5 = f32[1024]{0:T(1024)} fusion(bf16[384,1024]{1,0:T(8,128)(2,1)} %copy-done.10, f32[1024]{0:T(1024)S(1)} %copy-done.12, f32[384]{0:T(512)S(1)} %get-tuple-element.24), kind=kLoop, calls=%fused_computation.11 | loop fusion | flops 1571840 | bytes 796160 | tf_op jit(solution)/shard_map/reduce_sum | solution.py:279
  167.3 6.1 %fusion.6 = f32[1536,1024]{1,0:T(8,128)} fusion(bf16[384,768]{1,0:T(8,128)(2,1)} %copy-done.11, bf16[384,768]{1,0:T(8,128)(2,1)} %convolution_convert_fusion.3, bf16[384,1024]{1,0:T(8,128)(2,1)} %copy-done.10, f32[384]{0:T(512)S(1)} %get-tuple-element.25, f32[384]{0:T(512)S(1)} %get-tuple-element.24, f32[1024]{0:T(1024)S(1)} %mul.123), kind=kOutput, calls=%fused_computation.18 | convolution fusion | flops 1212284928 | bytes 8264704 | tf_op jit(solution)/shard_map/dot_general | solution.py:294
  173.5 5.4 %all-to-all-done.6 = bf16[8,48,1536]{2,1,0:T(8,128)(2,1)} async-done(((bf16[8,48,1536]{2,1,0:T(8,128)(2,1)}), bf16[8,48,1536]{2,1,0:T(8,128)(2,1)}, u32[]{:S(2)}, u32[]{:S(2)}) %all-to-all-start.6) | async-done | bytes 1179680 | tf_op jit(solution)/shard_map/all_to_all | solution.py:287
  178.9 2.2 %convert_reduce_fusion = f32[48,1536]{1,0:T(8,128)} fusion(bf16[8,48,1536]{2,1,0:T(8,128)(2,1)} %all-to-all-done.6), kind=kLoop, calls=%fused_computation.5 | loop fusion | flops 1105920 | bytes 1474560 | tf_op jit(solution)/shard_map/reduce_sum | solution.py:297
  (57 shorter events, 20.7 us)
Async XLA Ops:
  0.6 87.3 %copy-start = (bf16[1536,1024]{1,0:T(8,128)(2,1)S(1)}, bf16[1536,1024]{1,0:T(8,128)(2,1)}, u32[]{:S(2)}) copy-start(bf16[1536,1024]{1,0:T(8,128)(2,1)} %param.17) | copy-start | bytes 9437188
  3.2 1.3 copy-start.5
  4.5 1.3 copy-start.6
  6.7 20.8 %copy-start.7 = (bf16[48,8,768]{2,1,0:T(8,128)(2,1)}, bf16[48,8,768]{2,1,0:T(8,128)(2,1)S(1)}, u32[]{:S(2)}) copy-start(bf16[48,8,768]{2,1,0:T(8,128)(2,1)S(1)} %get-tuple-element.14) | copy-start | bytes 1769476
  27.5 22.0 %all-to-all-start.1 = ((bf16[8,6,8,768]{3,2,1,0:T(8,128)(2,1)}), bf16[8,6,8,768]{3,2,1,0:T(8,128)(2,1)}, u32[]{:S(2)}, u32[]{:S(2)}) async-start(bf16[8,6,8,768]{3,2,1,0:T(8,128)(2,1)} %bitcast.22), calls=%async_computation.1 | async-start | bytes 1179648 | tf_op jit(solution)/shard_map/all_to_all | solution.py:171
  31.8 1.2 copy-start.1
  33.0 1.9 %copy-start.3 = (bf16[2,1,1024,768]{3,2,1,0:T(8,128)(2,1)S(1)}, bf16[2,1,1024,768]{3,2,1,0:T(8,128)(2,1)}, u32[]{:S(2)}) copy-start(bf16[2,1,1024,768]{3,2,1,0:T(8,128)(2,1)} %cache.3) | copy-start | bytes 9437188
  48.6 0.8 copy-start.8
  50.4 20.5 %all-to-all-start.3 = ((bf16[8,48,896]{2,1,0:T(8,128)(2,1)}), bf16[8,48,896]{2,1,0:T(8,128)(2,1)}, u32[]{:S(2)}, u32[]{:S(2)}) async-start(bf16[8,48,896]{2,1,0:T(8,128)(2,1)} %broadcast_in_dim.10), calls=%async_computation.3 | async-start | bytes 1376256 | tf_op jit(solution)/shard_map/all_to_all | solution.py:222
  54.6 1.2 copy-start.2
  55.8 1.9 %copy-start.4 = (bf16[2,1,1024,768]{3,2,1,0:T(8,128)(2,1)S(1)}, bf16[2,1,1024,768]{3,2,1,0:T(8,128)(2,1)}, u32[]{:S(2)}) copy-start(bf16[2,1,1024,768]{3,2,1,0:T(8,128)(2,1)} %cache.3) | copy-start | bytes 9437188
  70.1 0.8 copy-start.9
  71.8 14.7 %all-to-all-start.4 = ((bf16[8,48,768]{2,1,0:T(8,128)(2,1)}), bf16[8,48,768]{2,1,0:T(8,128)(2,1)}, u32[]{:S(2)}, u32[]{:S(2)}) async-start(bf16[8,48,768]{2,1,0:T(8,128)(2,1)} %broadcast_in_dim.12), calls=%async_computation.4 | async-start | bytes 1179648 | tf_op jit(solution)/shard_map/all_to_all | solution.py:222
  88.0 3.6 %copy-start.11 = (bf16[384,768]{1,0:T(8,128)(2,1)}, bf16[384,768]{1,0:T(8,128)(2,1)S(1)}, u32[]{:S(2)}) copy-start(bf16[384,768]{1,0:T(8,128)(2,1)S(1)} %convolution_convert_fusion.2) | copy-start | bytes 1769476
  91.5 5.0 %copy-start.15 = (s32[384]{0:T(512)S(1)}, s32[384]{0:T(512)}, u32[]{:S(2)}) copy-start(s32[384]{0:T(512)} %param.15) | copy-start | bytes 4612
  91.5 5.5 %copy-start.12 = (f32[1024]{0:T(1024)S(1)}, f32[1024]{0:T(1024)}, u32[]{:S(2)}) copy-start(f32[1024]{0:T(1024)} %param.18) | copy-start | bytes 12292
  91.5 5.5 %copy-start.14 = (f32[1024]{0:T(1024)S(1)}, f32[1024]{0:T(1024)}, u32[]{:S(2)}) copy-start(f32[1024]{0:T(1024)} %param.19) | copy-start | bytes 12292
  91.5 22.5 %all-to-all-start.5 = ((bf16[4,96,1024]{2,1,0:T(8,128)(2,1)}), bf16[4,96,1024]{2,1,0:T(8,128)(2,1)}, u32[]{:S(2)}, u32[]{:S(2)}) async-start(bf16[4,96,1024]{2,1,0:T(8,128)(2,1)} %bitcast.25), calls=%async_computation.5 | async-start | bytes 1572864 | tf_op jit(solution)/shard_map/all_to_all | solution.py:257
  114.0 43.7 %all-to-all-start.2 = ((bf16[8,6,8,1536]{3,2,1,0:T(8,128)(2,1)}), bf16[8,6,8,1536]{3,2,1,0:T(8,128)(2,1)}, u32[]{:S(2)}, u32[]{:S(2)}) async-start(bf16[8,6,8,1536]{3,2,1,0:T(8,128)(2,1)} %bitcast.23), calls=%async_computation.2 | async-start | bytes 2359296 | tf_op jit(solution)/shard_map/all_to_all | solution.py:231
  139.0 0.9 copy-start.10
  153.0 4.8 %copy-start.13 = (f32[384]{0:T(512)}, f32[384]{0:T(512)S(1)}, u32[]{:S(2)}) copy-start(f32[384]{0:T(512)S(1)} %fusion.19) | copy-start | bytes 4612
  157.8 21.1 %all-to-all-start.6 = ((bf16[8,48,1536]{2,1,0:T(8,128)(2,1)}), bf16[8,48,1536]{2,1,0:T(8,128)(2,1)}, u32[]{:S(2)}, u32[]{:S(2)}) async-start(bf16[8,48,1536]{2,1,0:T(8,128)(2,1)} %bitcast.24), calls=%async_computation.6 | async-start | bytes 2359296 | tf_op jit(solution)/shard_map/all_to_all | solution.py:287
where the time goes:
time: 184 us; the launch traced here: 182 us
  blocking collectives  51.4 us (28%)
  Pallas kernels  29.7 us (16%)
  starting transfers between devices  26.6 us (14%)
  waiting for transfers between devices  26 us (14%)
  matrix products  17.3 us (9%)
  other arithmetic  15 us (8%)
  local copies, waits for them, and re-layouts  13.6 us (7%)
  between operations  2.61 us (1%)
    pallas_call x2, Pallas kernels, attend(): pl.pallas_call(functools.partial(attention_kernel, slot_count, placed), o...  26.1 us
    all_to_all x1, blocking collectives, shards(): lax.all_to_all(packed, 'dp', split_axis=0, concat_axis=0, tiled=True)  20.8 us
    all_gather x1, blocking collectives, shards(): lax.all_gather(part.astype(jnp.bfloat16), 'mp', axis=0, tiled=True)  17.9 us
    all_to_all x1, waiting for transfers between devices, shards(): lax.all_to_all(partial_mix.astype(jnp.bfloat16).reshape(planes, share, co...  14.7 us
    psum x1, blocking collectives, shards(): square_sum, signal = lax.psum((square_sum, signal), 'dp')  12.7 us
    unnamed x32, local copies, waits for them, and re-layouts  11.4 us
    all_to_all x2, starting transfers between devices, share_rows(): lax.all_to_all(copies, 'dp', split_axis=0, concat_axis=0, tiled=True)  8.39 us
    dot_general x1, matrix products, shards(): lax.dot_general(pooled_all, upstream_half, (((0,), (0,)), ((), ())), pref...  6.14 us
  transfers between devices with their start and end apart: 6, of which 3 were waited for; matrix products, arithmetic and copies ran while one was open for 13% of the time, Pallas kernels for 16%

commit v1 on v0

--- a/solution.py
+++ b/solution.py
@@ -112,7 +112,7 @@
     lax.fori_loop(0, out.shape[0], body, 0)
 
 
-def shards(
+def stepwise_shards(
     response_query,
     response_keys,
     prompt_cache,
@@ -298,6 +298,814 @@
     return (attention_rows, rewards, pair_loss, weight_gradient, head_gradient, pooled_gradient)
 
 
+MESH = pl.DeviceIdType.MESH
+NT = (((1,), (1,)), ((), ()))
+TN = (((0,), (0,)), ((), ()))
+
+
+def plan_kernel(per, chunk_slots, window, owners, lengths, query, keys, packed, info, target, count, got, held, sems):
+    me = lax.axis_index("dp")
+    groups = count.shape[0]
+    held_count = query.shape[0]
+    width = query.shape[2]
+    span = window * HD
+    first = jnp.minimum(
+        lax.axis_index("mp") * (width // HD) // (Q_HEADS // KV_HEADS), KV_HEADS - window
+    )
+    columns = pl.ds(pl.multiple_of(first * HD, HD), span)
+    loads = [
+        pltpu.make_async_copy(query, got, sems.at[0]),
+        pltpu.make_async_copy(keys.at[0, :, :, columns], held.at[0], sems.at[1]),
+        pltpu.make_async_copy(keys.at[1, :, :, columns], held.at[1], sems.at[2]),
+    ]
+    for load in loads:
+        load.start()
+    for owner in range(groups):
+        count[owner] = 0
+    spot = lax.broadcasted_iota(jnp.int32, (8, HD), 0) * HD + lax.broadcasted_iota(
+        jnp.int32, (8, HD), 1
+    )
+    block = groups * chunk_slots
+
+    def place(r, rows):
+        owner = owners[r]
+        j = count[owner]
+        count[owner] = j + 1
+        target[r] = owner * per + j
+        info[owner, pl.ds(j, 1), :] = jnp.full((1, HD), lengths[r], jnp.int32).astype(jnp.float32)
+        row = (
+            j // chunk_slots * (groups * block) + owner * block + j % chunk_slots * groups + me
+        )
+        return jnp.where(spot == me * held_count + r, row, rows)
+
+    rows = lax.fori_loop(0, held_count, place, jnp.zeros((8, HD), jnp.int32))
+    for owner in range(groups):
+        info[owner, pl.ds(8, 8), :] = rows.astype(jnp.float32)
+    for load in loads:
+        load.wait()
+
+    def move(r, carry):
+        p = target[r]
+        packed[p, :, pl.ds(0, width)] = got[r]
+        packed[p, :, pl.ds(width, span)] = held[0, r]
+        packed[p, :, pl.ds(width + span, span)] = held[1, r]
+        return carry
+
+    lax.fori_loop(0, held_count, move, 0)
+
+
+def layer_kernel(
+    sizes,
+    packed,
+    info,
+    cache,
+    weight,
+    residual,
+    gain,
+    head,
+    pairing,
+    returned,
+    pooled,
+    upstream,
+    reduced,
+    head_gradient,
+    rewards_out,
+    loss_out,
+    land,
+    info_land,
+    kv,
+    w,
+    res,
+    place,
+    sign,
+    shifted,
+    attended,
+    own,
+    z_send,
+    z_land,
+    z_total,
+    combined,
+    stat,
+    stat_land,
+    full_parts,
+    half_parts,
+    near_land,
+    far_send,
+    far_land,
+    load_sem,
+    info_sem,
+    move_sem,
+    local_sem,
+    pool_sem,
+    pass_sem,
+    back_sem,
+    z_sem,
+    t_sem,
+    stat_sem,
+    near_sem,
+    far_sem,
+):
+    groups, planes, per, chunk_slots, window, sub = sizes
+    me = lax.axis_index("dp")
+    rank = lax.axis_index("mp")
+    chips = groups // 2
+    chip = me // 2
+    core = me % 2
+    sibling = chip * 2 + 1 - core
+    chunks = per // chunk_slots
+    block = groups * chunk_slots
+    unit = chunk_slots * 8
+    rows = block * 8
+    mixed = groups * block
+    width = attended.shape[1]
+    local_heads = width // HD
+    group_size = Q_HEADS // KV_HEADS
+    stack = math.gcd(local_heads, group_size)
+    span = window * HD
+    count = pooled.shape[0]
+    first = jnp.minimum(rank * local_heads // group_size, KV_HEADS - window)
+    columns = pl.ds(pl.multiple_of(first * HD, HD), span)
+
+    def remote(src, dst, sem, index, **where):
+        return pltpu.make_async_remote_copy(
+            src_ref=src,
+            dst_ref=dst,
+            send_sem=sem.at[(0,) + index],
+            recv_sem=sem.at[(1,) + index],
+            device_id=where,
+            device_id_type=MESH,
+        )
+
+    def at(start, size):
+        return pl.ds(pl.multiple_of(start, size), size)
+
+    loads = [
+        pltpu.make_async_copy(cache.at[0, 0, :, columns], kv.at[0], load_sem.at[0]),
+        pltpu.make_async_copy(cache.at[1, 0, :, columns], kv.at[1], load_sem.at[1]),
+        pltpu.make_async_copy(residual, res, load_sem.at[2]),
+        pltpu.make_async_copy(weight, w, load_sem.at[3]),
+    ]
+    for load in loads:
+        load.start()
+
+    barrier = pltpu.get_barrier_semaphore()
+    for d in range(1, groups):
+        pl.semaphore_signal(
+            barrier, inc=1, device_id={"dp": (me + d) % groups}, device_id_type=MESH
+        )
+    for d in range(1, planes):
+        pl.semaphore_signal(
+            barrier, inc=1, device_id={"mp": (rank + d) % planes}, device_id_type=MESH
+        )
+    pl.semaphore_wait(barrier, groups + planes - 2)
+
+    infos = []
+    for d in range(1, groups):
+        peer = (me + d) % groups
+        copy = remote(info.at[peer], info_land.at[me], info_sem, (d - 1,), dp=peer)
+        copy.start()
+        infos.append(copy)
+    moves = []
+    locals_ = []
+    for c in range(chunks):
+        moves.append([])
+        for d in range(1, groups):
+            peer = (me + d) % groups
+            copy = remote(
+                packed.at[at((peer * chunks + c) * unit, unit), :],
+                land.at[at((c * groups + me) * unit, unit), :],
+                move_sem,
+                (c * (groups - 1) + d - 1,),
+                dp=peer,
+            )
+            copy.start()
+            moves[c].append(copy)
+        copy = pltpu.make_async_copy(
+            packed.at[at((me * chunks + c) * unit, unit), :],
+            land.at[at((c * groups + me) * unit, unit), :],
+            local_sem.at[c],
+        )
+        copy.start()
+        locals_.append(copy)
+
+    info_land[me] = info[me]
+    for copy in infos:
+        copy.wait_recv()
+    row_of = info_land[0, pl.ds(8, 8), :]
+    for g in range(1, groups):
+        row_of = row_of + info_land[g, pl.ds(8, 8), :]
+    row_of = row_of.astype(jnp.int32)
+    row_at = lax.broadcasted_iota(jnp.int32, (count, HD), 0)
+    for a in range(count // HD):
+        place[:, a * HD : (a + 1) * HD] = jnp.where(
+            row_at == row_of[a : a + 1, :], 1.0, 0.0
+        ).astype(jnp.bfloat16)
+    asked = jnp.where(
+        lax.broadcasted_iota(jnp.int32, (count, count), 0) == pairing[...], 1.0, 0.0
+    ).astype(jnp.bfloat16)
+    pair = lax.broadcasted_iota(jnp.int32, (count // 2, count), 0) * 2
+    entry = lax.broadcasted_iota(jnp.int32, (count // 2, count), 1)
+    side = jnp.where(entry == pair, 1.0, jnp.where(entry == pair + 1, -1.0, 0.0))
+    chosen = lax.dot_general(
+        side.astype(jnp.bfloat16), asked, NT, preferred_element_type=jnp.float32
+    )
+    sign[...] = lax.dot_general(
+        chosen.astype(jnp.bfloat16), place[...], NT, preferred_element_type=jnp.float32
+    )
+    loads[2].wait()
+    shifted[...] = jnp.dot(place[...], res[...], preferred_element_type=jnp.float32)
+
+    scale = math.log2(math.e) / math.sqrt(HD)
+    tall = stack * rows
+
+    def attend(c):
+        here = pl.ds(c * rows, rows)
+        row = lax.broadcasted_iota(jnp.int32, (tall, rows), 0) % rows
+        col = lax.broadcasted_iota(jnp.int32, (tall, rows), 1)
+        causal = (row // 8 == col // 8) & (col <= row)
+        for s in range(local_heads // stack):
+            part = (rank * local_heads + stack * s) // group_size - first
+            query = jnp.concatenate(
+                [
+                    land[here, h * HD : (h + 1) * HD]
+                    for h in range(s * stack, (s + 1) * stack)
+                ],
+                axis=0,
+            )
+            own_k = land[here, pl.ds(pl.multiple_of(width + part * HD, HD), HD)]
+            own_v = land[here, pl.ds(pl.multiple_of(width + span + part * HD, HD), HD)]
+            key = kv[0, :, pl.ds(pl.multiple_of(part * HD, HD), HD)]
+            value = kv[1, :, pl.ds(pl.multiple_of(part * HD, HD), HD)]
+            far = lax.dot_general(query, key, NT, preferred_element_type=jnp.float32)
+            near = lax.dot_general(query, own_k, NT, preferred_element_type=jnp.float32)
+            near = jnp.where(causal, near, -1e30)
+            top = jnp.maximum(
+                jnp.max(far, axis=1, keepdims=True), jnp.max(near, axis=1, keepdims=True)
+            )
+            far = jnp.exp2((far - top) * scale).astype(jnp.bfloat16)
+            near = jnp.exp2((near - top) * scale).astype(jnp.bfloat16)
+            ones = lambda v: jnp.concatenate([v, jnp.ones_like(v)], axis=1)
+            both = jnp.dot(far, ones(value), preferred_element_type=jnp.float32)
+            both += jnp.dot(near, ones(own_v), preferred_element_type=jnp.float32)
+            out = (both[:, :HD] / both[:, HD:]).astype(jnp.bfloat16)
+            for h in range(stack):
+                attended[here, (s * stack + h) * HD : (s * stack + h + 1) * HD] = out[
+                    h * rows : (h + 1) * rows
+                ]
+
+    pools = []
+    passes = []
+
+    def share(c):
+        slots = [
+            jnp.concatenate(
+                [info_land[g, pl.ds(c * chunk_slots + k, 1), :] for g in range(groups)], axis=0
+            )
+            for k in range(chunk_slots)
+        ]
+        length = jnp.concatenate(slots, axis=0).astype(jnp.int32)
+        i = lax.broadcasted_iota(jnp.int32, (block, HD), 0)
+        col = lax.broadcasted_iota(jnp.int32, (block, HD), 1)
+        start = (i % groups * chunk_slots + i // groups) * 8 - 1
+        pick = jnp.where(col == start + length, 1.0, 0.0).astype(jnp.bfloat16)
+        last = jnp.dot(
+            pick, attended[pl.ds(c * rows, rows), :], preferred_element_type=jnp.float32
+        )
+        mine = at(c * mixed + me * block, block)
+        pooled[mine, :] = last.astype(jnp.bfloat16)
+        sent = []
+        for q in range(1, chips):
+            sent.append(
+                remote(
+                    pooled.at[mine, :],
+                    pooled.at[mine, :],
+                    pool_sem,
+                    (c * chips + q,),
+                    dp=(chip + q) % chips * 2 + core,
+                )
+            )
+        sent.append(
+            remote(
+                pooled.at[mine, :], pooled.at[mine, :], pool_sem, (c * chips,), dp=sibling
+            )
+        )
+        for copy in sent:
+            copy.start()
+        pools.append(sent)
+
+    def pass_on(c):
+        sent = []
+        for q in range(1, chips):
+            pools[c][q - 1].wait_recv()
+            source = (chip + chips - q) % chips * 2 + core
+            there = at(c * mixed + source * block, block)
+            copy = remote(
+                pooled.at[there, :],
+                pooled.at[there, :],
+                pass_sem,
+                (c * (chips - 1) + q - 1,),
+                dp=sibling,
+            )
+            copy.start()
+            sent.append(copy)
+        passes.append(sent)
+
+    depth = jnp.minimum(rank, planes - 1 - rank)
+    centre = planes // 2 - 1
+    is_centre = depth == centre
+    low = rank < planes // 2
+    inward = jnp.where(low, rank + 1, rank - 1)
+    outward = jnp.where(low, rank - 1, rank + 1)
+    outward = jnp.where(depth == 0, inward, outward)
+    slot = jnp.where(is_centre, 1, 0)
+    steps = mixed // sub
+    z_copies = [
+        remote(
+            z_send.at[pl.ds(n * sub, sub), :],
+            z_land.at[slot, pl.ds(n * sub, sub), :],
+            z_sem,
+            (slot, n),
+            mp=inward,
+        )
+        for n in range(chunks * steps)
+    ]
+    z_waits = [
+        [
+            remote(
+                z_send.at[pl.ds(n * sub, sub), :],
+                z_land.at[k, pl.ds(n * sub, sub), :],
+                z_sem,
+                (k, n),
+                mp=inward,
+            )
+            for n in range(chunks * steps)
+        ]
+        for k in range(2)
+    ]
+    t_copies = [
+        remote(
+            z_total.at[pl.ds(n * sub, sub), :],
+            z_total.at[pl.ds(n * sub, sub), :],
+            t_sem,
+            (n,),
+            mp=outward,
+        )
+        for n in range(chunks * steps)
+    ]
+
+    def mix(c):
+        for copy in passes[c]:
+            copy.wait_recv()
+        pools[c][-1].wait_recv()
+        if c == 0:
+            loads[3].wait()
+        here = pl.ds(c * mixed, mixed)
+        product = jnp.dot(pooled[here, :], w[...], preferred_element_type=jnp.float32)
+        own[here, :] = product
+        z_send[here, :] = product.astype(jnp.bfloat16)
+
+        @pl.when(depth == 0)
+        def _():
+            for n in range(c * steps, (c + 1) * steps):
+                z_copies[n].start()
+
+    def inner(n):
+        here = pl.ds(n * sub, sub)
+
+        @pl.when(depth > 0)
+        def _():
+            z_waits[0][n].wait_recv()
+            z_send[here, :] = (own[here, :] + z_land[0, here, :].astype(jnp.float32)).astype(
+                jnp.bfloat16
+            )
+            z_copies[n].start()
+
+    scaled_head = gain[...] * head[...]
+
+    def finish(n):
+        here = pl.ds(n * sub, sub)
+
+        @pl.when(is_centre)
+        def _():
+            z_waits[1][n].wait_recv()
+            z_total[here, :] = (
+                z_send[here, :].astype(jnp.float32) + z_land[1, here, :].astype(jnp.float32)
+            ).astype(jnp.bfloat16)
+
+        @pl.when(depth < centre)
+        def _():
+            t_copies[n].wait_recv()
+
+        @pl.when(depth > 0)
+        def _():
+            t_copies[n].start()
+
+        whole = z_total[here, :].astype(jnp.float32) + shifted[here, :]
+        combined[here, :] = whole
+        square = jnp.sum(whole * whole, axis=1, keepdims=True)
+        signal = jnp.sum(whole * scaled_head, axis=1, keepdims=True)
+        lane = lax.broadcasted_iota(jnp.int32, (sub, HD), 1)
+        this = lax.broadcasted_iota(jnp.int32, (sub, HD), 0) + n * sub % HD
+        line = n * sub // HD
+        for k, column in enumerate((square, signal)):
+            spread = jnp.sum(jnp.where(lane == this, column, 0.0), axis=0, keepdims=True)
+            there = pl.ds(k * (count // HD) + line, 1)
+            if n * sub % HD == 0:
+                stat[there, :] = spread
+            else:
+                stat[there, :] += spread
+
+    backs = []
+
+    def give_back(c):
+        for d in range(1, groups):
+            peer = (me + d) % groups
+            copy = remote(
+                attended.at[at((c * groups + peer) * unit, unit), :],
+                returned.at[at((me * chunks + c) * unit, unit), :],
+                back_sem,
+                (c * (groups - 1) + d - 1,),
+                dp=peer,
+            )
+            copy.start()
+            backs.append(copy)
+        copy = pltpu.make_async_copy(
+            attended.at[at((c * groups + me) * unit, unit), :],
+            returned.at[at((me * chunks + c) * unit, unit), :],
+            local_sem.at[chunks + c],
+        )
+        copy.start()
+        locals_.append(copy)
+
+    for c in range(chunks):
+        for copy in moves[c]:
+            copy.wait_recv()
+        locals_[c].wait()
+        if c == 0:
+            loads[0].wait()
+            loads[1].wait()
+        attend(c)
+        share(c)
+        if c > 0:
+            pass_on(c - 1)
+            mix(c - 1)
+    taken = (chunks - 2) * steps
+    for n in range(taken):
+        inner(n)
+    pass_on(chunks - 1)
+    for c in range(chunks):
+        give_back(c)
+    mix(chunks - 1)
+    total = chunks * steps
+    done = 0
+    for n in range(taken, total):
+        inner(n)
+        while done < n - 1 + (n == total - 1):
+            finish(done)
+            done += 1
+    while done < total:
+        finish(done)
+        done += 1
+
+    lines = count // HD
+    stat[pl.ds(2 * lines, 8 - 2 * lines), :] = jnp.zeros((8 - 2 * lines, HD), jnp.float32)
+    stats = []
+    for d in range(1, groups):
+        copy = remote(stat, stat_land.at[me], stat_sem, (d - 1,), dp=(me + d) % groups)
+        copy.start()
+        stats.append(copy)
+    stat_land[me] = stat[...]
+    for copy in stats:
+        copy.wait_recv()
+    sums = stat_land[0]
+    for g in range(1, groups):
+        sums = sums + stat_land[g]
+    square_sum = jnp.concatenate([sums[a : a + 1] for a in range(lines)], axis=1)
+    signal = jnp.concatenate([sums[lines + a : lines + a + 1] for a in range(lines)], axis=1)
+    inverse = lax.rsqrt(square_sum / D + EPSILON)
+    rewards = inverse * signal
+    margin = jnp.sum(sign[...] * rewards, axis=1, keepdims=True)
+    pairs = count // 2
+    slope = -jax.nn.sigmoid(-margin) / pairs
+    reward_slope = jnp.sum(sign[...] * slope, axis=0, keepdims=True)
+    direct = reward_slope * inverse
+    norm = direct * inverse * inverse * signal / D
+    eye = lax.broadcasted_iota(jnp.int32, (HD, HD), 0) == lax.broadcasted_iota(
+        jnp.int32, (HD, HD), 1
+    )
+
+    def upright(line):
+        return jnp.concatenate(
+            [
+                jnp.sum(
+                    jnp.where(eye, line[:, a * HD : (a + 1) * HD], 0.0), axis=1, keepdims=True
+                )
+                for a in range(lines)
+            ],
+            axis=0,
+        )
+
+    direct_rows = upright(direct)
+    norm_rows = upright(norm)
+    nears = []
+    for c in range(chunks):
+        here = pl.ds(c * mixed, mixed)
+        upstream[here, :] = (
+            direct_rows[c * mixed : (c + 1) * mixed] * scaled_head
+            - norm_rows[c * mixed : (c + 1) * mixed] * combined[here, :]
+        ).astype(jnp.bfloat16)
+        slopes = lax.dot_general(
+            upstream[here, :], w[...], NT, preferred_element_type=jnp.float32
+        ).reshape(block, groups, width)
+        there = pl.ds(c * block, block)
+        for g in range(groups):
+            full_parts[g % 2, g // 2, there, :] = slopes[:, g, :]
+            half_parts[g % 2, g // 2, there, :] = slopes[:, g, :].astype(jnp.bfloat16)
+        copy = remote(
+            half_parts.at[1 - core, :, there, :],
+            near_land.at[:, there, :],
+            near_sem,
+            (c,),
+            dp=sibling,
+        )
+        copy.start()
+        nears.append(copy)
+
+    fars = []
+    for c in range(chunks):
+        there = pl.ds(c * block, block)
+        nears[c].wait_recv()
+        for q in range(chips):
+            goal = (chip + q) % chips
+            both = full_parts[core, goal, there, :] + near_land[goal, there, :].astype(jnp.float32)
+            if q == 0:
+                reduced[there, :] = both
+            else:
+                far_send[q - 1, there, :] = both.astype(jnp.bfloat16)
+                copy = remote(
+                    far_send.at[q - 1, there, :],
+                    far_land.at[q - 1, there, :],
+                    far_sem,
+                    (c * (chips - 1) + q - 1,),
+                    dp=goal * 2 + core,
+                )
+                copy.start()
+                fars.append(copy)
+
+    rewards_rows = upright(rewards)
+    rewards_out[...] = jnp.sum(
+        place[...].astype(jnp.float32) * rewards_rows, axis=0, keepdims=True
+    )
+    against = -margin
+    soft = jnp.maximum(against, 0.0) + jnp.log1p(jnp.exp(-jnp.abs(against)))
+    loss_out[...] = jnp.sum(soft, axis=0, keepdims=True) / pairs
+    head_gradient[...] = jnp.sum(direct_rows * combined[...], axis=0, keepdims=True) * gain[...]
+
+    for c in range(chunks):
+        there = pl.ds(c * block, block)
+        extra = None
+        for q in range(1, chips):
+            fars[c * (chips - 1) + q - 1].wait_recv()
+            piece = far_land[q - 1, there, :].astype(jnp.float32)
+            extra = piece if extra is None else extra + piece
+        reduced[there, :] += extra
+
+    for copy in backs:
+        copy.wait_recv()
+    for copy in locals_[chunks:]:
+        copy.wait()
+    sent = infos + backs + stats + nears + fars
+    for group in moves + pools + passes:
+        sent = sent + group
+    for copy in sent + z_copies:
+        copy.wait_send()
+
+    @pl.when(depth > 0)
+    def _():
+        for copy in t_copies:
+            copy.wait_send()
+
+
+def gradient_kernel(per, chunk_slots, target, lengths, returned, reduced, pooled, upstream, rows_out, pooled_gradient, weight_gradient):
+    groups = returned.shape[0] // per
+    block = groups * chunk_slots
+
+    @pl.when(pl.program_id(0) == 0)
+    def _():
+        token = lax.broadcasted_iota(jnp.int32, returned.shape[1:], 0)
+
+        def body(r, carry):
+            p = target[r]
+            rows_out[r] = jnp.where(token < lengths[r], returned[p], jnp.zeros_like(returned[p]))
+            owner = p // per
+            j = p % per
+            row = j // chunk_slots * block + owner * chunk_slots + j % chunk_slots
+            pooled_gradient[pl.ds(r, 1), :] = reduced[pl.ds(row, 1), :]
+            return carry
+
+        lax.fori_loop(0, rows_out.shape[0], body, 0)
+
+    weight_gradient[...] = lax.dot_general(
+        pooled[...], upstream[...], TN, preferred_element_type=jnp.float32
+    )
+
+
+def fused_shards(
+    response_query,
+    response_keys,
+    prompt_cache,
+    lengths,
+    owners,
+    pairing,
+    residual,
+    output_weight,
+    norm_gain,
+    reward_head,
+):
+    groups = lax.axis_size("dp")
+    planes = lax.axis_size("mp")
+    held_count, slot_count, width = response_query.shape
+    local_heads = width // HD
+    group_size = Q_HEADS // KV_HEADS
+    per = held_count // groups
+    count = held_count * groups
+    columns = output_weight.shape[1]
+    prefix = prompt_cache.shape[2]
+    window = kv_window(planes, local_heads)
+    chunk_slots = slots_of_chunk(groups, per)
+    chunks = per // chunk_slots
+    block = groups * chunk_slots
+    chips = groups // 2
+    span = window * HD
+    packed_width = width + 2 * span
+    bf16, f32 = jnp.bfloat16, jnp.float32
+    vmem = pl.BlockSpec(memory_space=pltpu.VMEM)
+    smem = pl.BlockSpec(memory_space=pltpu.SMEM)
+    hbm = pl.BlockSpec(memory_space=pl.ANY)
+    packed, info, target = pl.pallas_call(
+        functools.partial(plan_kernel, per, chunk_slots, window),
+        out_shape=(
+            jax.ShapeDtypeStruct((held_count, slot_count, packed_width), bf16),
+            jax.ShapeDtypeStruct((groups, 16, HD), f32),
+            jax.ShapeDtypeStruct((held_count,), jnp.int32),
+        ),
+        in_specs=[smem, smem, hbm, hbm],
+        out_specs=(vmem, vmem, smem),
+        scratch_shapes=[
+            pltpu.SMEM((groups,), jnp.int32),
+            pltpu.VMEM((held_count, slot_count, width), bf16),
+            pltpu.VMEM((2, held_count, slot_count, span), bf16),
+            pltpu.SemaphoreType.DMA((3,)),
+        ],
+        compiler_params=pltpu.CompilerParams(vmem_limit_bytes=16 << 20),
+        name="plan",
+    )(owners, lengths, response_query, response_keys)
+    slots = held_count * slot_count
+    sub = SUB
+    steps = count // sub
+    dma = lambda *shape: pltpu.SemaphoreType.DMA(shape)
+    returned, pooled, upstream, reduced, head_gradient, rewards, loss = pl.pallas_call(
+        functools.partial(
+            layer_kernel, (groups, planes, per, chunk_slots, window, sub)
+        ),
+        out_shape=(
+            jax.ShapeDtypeStruct((slots, width), bf16),
+            jax.ShapeDtypeStruct((count, width), bf16),
+            jax.ShapeDtypeStruct((count, columns), bf16),
+            jax.ShapeDtypeStruct((held_count, width), f32),
+            jax.ShapeDtypeStruct((1, columns), f32),
+            jax.ShapeDtypeStruct((1, count), f32),
+            jax.ShapeDtypeStruct((1, 1), f32),
+        ),
+        in_specs=[vmem, vmem, hbm, hbm, hbm, vmem, vmem, vmem],
+        out_specs=(vmem,) * 7,
+        scratch_shapes=[
+            pltpu.VMEM((slots, packed_width), bf16),
+            pltpu.VMEM((groups, 16, HD), f32),
+            pltpu.VMEM((2, prefix, span), bf16),
+            pltpu.VMEM((width, columns), bf16),
+            pltpu.VMEM((count, columns), bf16),
+            pltpu.VMEM((count, count), bf16),
+            pltpu.VMEM((count // 2, count), f32),
+            pltpu.VMEM((count, columns), f32),
+            pltpu.VMEM((slots, width), bf16),
+            pltpu.VMEM((count, columns), f32),
+            pltpu.VMEM((count, columns), bf16),
+            pltpu.VMEM((2, count, columns), bf16),
+            pltpu.VMEM((count, columns), bf16),
+            pltpu.VMEM((count, columns), f32),
+            pltpu.VMEM((8, HD), f32),
+            pltpu.VMEM((groups, 8, HD), f32),
+            pltpu.VMEM((2, chips, held_count, width), f32),
+            pltpu.VMEM((2, chips, held_count, width), bf16),
+            pltpu.VMEM((chips, held_count, width), bf16),
+            pltpu.VMEM((chips - 1, held_count, width), bf16),
+            pltpu.VMEM((chips - 1, held_count, width), bf16),
+            dma(4),
+            dma(2, groups - 1),
+            dma(2, chunks * (groups - 1)),
+            dma(2 * chunks),
+            dma(2, chunks * chips),
+            dma(2, chunks * (chips - 1)),
+            dma(2, chunks * (groups - 1)),
+            dma(2, 2, steps),
+            dma(2, steps),
+            dma(2, groups - 1),
+            dma(2, chunks),
+            dma(2, chunks * (chips - 1)),
+        ],
+        compiler_params=pltpu.CompilerParams(
+            collective_id=0, has_side_effects=True, vmem_limit_bytes=44 << 20
+        ),
+        name="layer",
+    )(
+        packed.reshape(slots, packed_width),
+        info,
+        prompt_cache,
+        output_weight,
+        residual,
+        norm_gain[None],
+        reward_head[None],
+        pairing[None],
+    )
+    tile = 256
+    attention_rows, pooled_gradient, weight_gradient = pl.pallas_call(
+        functools.partial(gradient_kernel, per, chunk_slots),
+        out_shape=(
+            jax.ShapeDtypeStruct(response_query.shape, bf16),
+            jax.ShapeDtypeStruct((held_count, width), f32),
+            jax.ShapeDtypeStruct((width, columns), f32),
+        ),
+        grid=(width // tile,),
+        in_specs=[
+            smem,
+            smem,
+            pl.BlockSpec((held_count, slot_count, width), lambda i: (0, 0, 0)),
+            pl.BlockSpec((held_count, width), lambda i: (0, 0)),
+            pl.BlockSpec((count, tile), lambda i: (0, i)),
+            pl.BlockSpec((count, columns), lambda i: (0, 0)),
+        ],
+        out_specs=(
+            pl.BlockSpec((held_count, slot_count, width), lambda i: (0, 0, 0)),
+            pl.BlockSpec((held_count, width), lambda i: (0, 0)),
+            pl.BlockSpec((tile, columns), lambda i: (i, 0)),
+        ),
+        compiler_params=pltpu.CompilerParams(vmem_limit_bytes=32 << 20),
+        name="gradient",
+    )(
+        target,
+        lengths,
+        returned.reshape(held_count, slot_count, width),
+        reduced,
+        pooled,
+        upstream,
+    )
+    return (
+        attention_rows,
+        rewards[0],
+        loss[0, 0],
+        weight_gradient,
+        head_gradient[0],
+        pooled_gradient,
+    )
+
+
+SUB = 64
+
+
+def kv_window(planes, local_heads):
+    group_size = Q_HEADS // KV_HEADS
+    return max(
+        (m * local_heads + local_heads - 1) // group_size - m * local_heads // group_size + 1
+        for m in range(planes)
+    )
+
+
+def slots_of_chunk(groups, per):
+    for slots in range(1, per + 1):
+        if per % slots == 0 and slots * groups % 16 == 0:
+            return slots
+    return 0
+
+
+def fits(shape, responses):
+    groups, planes = shape["dp"], shape["mp"]
+    held = responses // groups
+    if held % groups or groups % 2 or planes % 2:
+        return False
+    slots = slots_of_chunk(groups, held // groups)
+    return bool(slots) and slots * groups * 8 == HD and responses % HD == 0 and responses <= 3 * HD
+
+
+def shards(*args):
+    held = args[0].shape[0]
+    groups = lax.axis_size("dp")
+    sizes = {"dp": groups, "mp": lax.axis_size("mp")}
+    if fits(sizes, held * groups):
+        return fused_shards(*args)
+    return stepwise_shards(*args)
+
+
 def solution(mesh):
     placed = (
         P("dp", None, "mp"),

time: 184 us -> 99.2 us (0.54)
  Pallas kernels: 29.7 us -> 89.5 us
  blocking collectives: 51.4 us -> 0 us
  starting transfers between devices: 26.6 us -> 0 us
  waiting for transfers between devices: 26 us -> 0 us
  matrix products: 17.3 us -> 0 us
  other arithmetic: 15 us -> 0.6 us
  local copies, waits for them, and re-layouts: 13.6 us -> 6.34 us
    pallas_call x4 -> x3, Pallas kernels: 29.7 us -> 89.5 us  [the longest x1 79.9 us: fused_shards(): pl.pallas_call(functools.partial(layer_kernel, (groups, planes, per, chun...]
    all_to_all x6 -> x0, starting transfers between devices: 26.6 us -> none  [the longest x2 8.39 us: share_rows(): lax.all_to_all(copies, 'dp', split_axis=0, concat_axis=0, tiled=True)]
    all_to_all x6 -> x0, waiting for transfers between devices: 26 us -> none  [the longest x1 14.7 us: shards(): lax.all_to_all(partial_mix.astype(jnp.bfloat16).reshape(planes, share, co...]
    all_to_all x1 -> x0, blocking collectives: 20.8 us -> none  [shards(): lax.all_to_all(packed, 'dp', split_axis=0, concat_axis=0, tiled=True)]
    all_gather x1 -> x0, blocking collectives: 17.9 us -> none  [shards(): lax.all_gather(part.astype(jnp.bfloat16), 'mp', axis=0, tiled=True)]
    dot_general x5 -> x0, matrix products: 17.3 us -> none  [the longest x1 6.14 us: shards(): lax.dot_general(pooled_all, upstream_half, (((0,), (0,)), ((), ())), pref...]
    psum x1 -> x0, blocking collectives: 12.7 us -> none  [shards(): square_sum, signal = lax.psum((square_sum, signal), 'dp')]
    reduce_sum x8 -> x0, other arithmetic: 7.97 us -> none  [the longest x1 2.17 us: shards(): pooled_gradient = jnp.sum(slope_parts.astype(jnp.float32), axis=0)]
  transfers between devices with their start and end apart: 6 -> 0, of which waited for: 3 -> 0; matrix products, arithmetic and copies ran while one was open for 13% -> 0% of each run, Pallas kernels for 16% -> 0%
where the time goes in v1:
time: 99.2 us; the launch traced here: 98.9 us
  Pallas kernels  89.5 us (90%)
  local copies, waits for them, and re-layouts  6.34 us (6%)
  between operations  2.49 us (3%)
    pallas_call x1, Pallas kernels, fused_shards(): pl.pallas_call(functools.partial(layer_kernel, (groups, planes, per, chun...  79.9 us
    pallas_call x1, Pallas kernels, fused_shards(): pl.pallas_call(functools.partial(gradient_kernel, per, chunk_slots), out_...  6.95 us
    unnamed x21, local copies, waits for them, and re-layouts  6.34 us
    pallas_call x1, Pallas kernels, fused_shards(): pl.pallas_call(functools.partial(plan_kernel, per, chunk_slots, window),...  2.65 us

profile of v1, /device:TPU:0, one launch (start us, length us, event | category | flops | bytes accessed | tf_op | source)
XLA Modules:
  0.0 98.9 jit_solution(13689584249301632671)
XLA Ops:
  0.6 0.0 copy-start.1
  0.6 1.3 %copy-done.1 = bf16[48,8,1536]{2,1,0:T(8,128)(2,1)S(1)} copy-done((bf16[48,8,1536]{2,1,0:T(8,128)(2,1)S(1)}, bf16[48,8,1536]{2,1,0:T(8,128)(2,1)}, u32[]{:S(2)}) %copy-start.1) | copy-done | bytes 1179672
  1.9 0.0 copy-start.2
  1.9 1.3 %copy-done.2 = bf16[2,48,8,768]{3,2,1,0:T(8,128)(2,1)S(1)} copy-done((bf16[2,48,8,768]{3,2,1,0:T(8,128)(2,1)S(1)}, bf16[2,48,8,768]{3,2,1,0:T(8,128)(2,1)}, u32[]{:S(2)}) %copy-start.2) | copy-done | bytes 1179672
  3.2 0.0 copy-start.6
  3.2 0.7 copy-done.6
  3.8 0.0 copy-start.8
  3.8 0.7 copy-done.8
  4.5 0.0 copy-start.9
  4.5 0.0 copy-start.3
  4.5 0.0 copy-start.4
  4.5 0.0 copy-start.5
  4.5 2.6 %plan.1 = (bf16[48,8,2048]{2,1,0:T(8,128)(2,1)S(1)}, f32[8,16,128]{2,1,0:T(8,128)S(1)}, s32[48]{0:T(128)S(1)}) custom-call(s32[48]{0:T(128)S(1)} %copy-done.8, s32[48]{0:T(128)S(1)} %copy-done.6, bf16[48,8,1536]{2,1,0:T(8,128)(2,1)S(1)} %copy-done.1, bf16[2,48,8,768]{3,2,1,0:T(8,128)(2,1)S(1)} %copy-done.2), custom_call_target="tpu_custom_call" | custom-call | tf_op jit(solution)/shard_map/plan/pallas_call | solution.py:945
  7.2 0.0 copy-done.9
  7.2 0.0 copy-done.3
  7.2 0.0 copy-done.4
  7.2 0.0 copy-done.5
  7.2 0.0 copy-start
  7.2 1.9 %copy-done = bf16[2,1,1024,768]{3,2,1,0:T(8,128)(2,1)S(1)} copy-done((bf16[2,1,1024,768]{3,2,1,0:T(8,128)(2,1)S(1)}, bf16[2,1,1024,768]{3,2,1,0:T(8,128)(2,1)}, u32[]{:S(2)}) %copy-start) | copy-done | bytes 3145752
  9.1 79.9 %layer.1 = (bf16[384,1536]{1,0:T(8,128)(2,1)S(1)}, bf16[384,1536]{1,0:T(8,128)(2,1)S(1)}, bf16[384,1024]{1,0:T(8,128)(2,1)S(1)}, f32[48,1536]{1,0:T(8,128)S(1)},...) custom-call(bf16[384,2048]{1,0:T(8,128)(2,1)S(1)} %bitcast.6, ...), custom_call_target="tpu_custom_call" | custom-call | tf_op jit(solution)/shard_map/layer/pallas_call | solution.py:967
  89.0 0.0 copy-done.7
  89.0 6.9 %gradient.1 = (bf16[48,8,1536]{2,1,0:T(8,128)(2,1)}, f32[48,1536]{1,0:T(8,128)}, f32[1536,1024]{1,0:T(8,128)}) custom-call(s32[48]{0:T(128)S(1)} %get-tuple-element.19.target, s32[48]{0:T(128)S(1)} %copy-done.7, bf16[48,8,1536]{2,1,0:T(8,128)(2,1)S(1)} %bitcast.7, f32[48,1536]{1,0:T(8,128)S(1)} %get-tuple-element.23.reduced, ...), custom_call_target="tpu_custom_call" | custom-call | tf_op jit(solution)/shard_map/gradient/pallas_call | solution.py:1032
  96.0 0.6 reduce
  97.2 0.6 copy.19
  (2 shorter events, 0.0 us)
Async XLA Ops:
  0.6 1.3 %copy-start.1 = (bf16[48,8,1536]{2,1,0:T(8,128)(2,1)S(1)}, bf16[48,8,1536]{2,1,0:T(8,128)(2,1)}, u32[]{:S(2)}) copy-start(bf16[48,8,1536]{2,1,0:T(8,128)(2,1)} %query.1) | copy-start | bytes 3538948
  1.9 1.3 %copy-start.2 = (bf16[2,48,8,768]{3,2,1,0:T(8,128)(2,1)S(1)}, bf16[2,48,8,768]{3,2,1,0:T(8,128)(2,1)}, u32[]{:S(2)}) copy-start(bf16[2,48,8,768]{3,2,1,0:T(8,128)(2,1)} %keys.1) | copy-start | bytes 3538948
  3.2 0.7 copy-start.6
  3.8 0.7 copy-start.8
  4.5 2.7 %copy-start.9 = (s32[384]{0:T(512)S(1)}, s32[384]{0:T(512)}, u32[]{:S(2)}) copy-start(s32[384]{0:T(512)} %param.15) | copy-start | bytes 4612
  4.5 2.7 %copy-start.3 = (bf16[384,1024]{1,0:T(8,128)(2,1)S(1)}, bf16[384,1024]{1,0:T(8,128)(2,1)}, u32[]{:S(2)}) copy-start(bf16[384,1024]{1,0:T(8,128)(2,1)} %residual.1) | copy-start | bytes 2359300
  4.5 2.7 %copy-start.4 = (f32[1024]{0:T(1024)S(1)}, f32[1024]{0:T(1024)}, u32[]{:S(2)}) copy-start(f32[1024]{0:T(1024)} %param.18) | copy-start | bytes 12292
  4.5 2.7 %copy-start.5 = (f32[1024]{0:T(1024)S(1)}, f32[1024]{0:T(1024)}, u32[]{:S(2)}) copy-start(f32[1024]{0:T(1024)} %param.19) | copy-start | bytes 12292
  7.2 1.9 %copy-start = (bf16[2,1,1024,768]{3,2,1,0:T(8,128)(2,1)S(1)}, bf16[2,1,1024,768]{3,2,1,0:T(8,128)(2,1)}, u32[]{:S(2)}) copy-start(bf16[2,1,1024,768]{3,2,1,0:T(8,128)(2,1)} %cache.1) | copy-start | bytes 9437188
  9.1 79.9 %copy-start.7 = (s32[48]{0:T(128)S(1)}, s32[48]{0:T(128)}, u32[]{:S(2)}) copy-start(s32[48]{0:T(128)} %lengths.3) | copy-start | bytes 580

commit v2 on v1

--- a/solution.py
+++ b/solution.py
@@ -378,6 +378,7 @@
     res,
     place,
     sign,
+    turn,
     shifted,
     attended,
     own,
@@ -387,8 +388,8 @@
     combined,
     stat,
     stat_land,
-    full_parts,
-    half_parts,
+    turned,
+    near_send,
     near_land,
     far_send,
     far_land,
@@ -406,6 +407,7 @@
     far_sem,
 ):
     groups, planes, per, chunk_slots, window, sub = sizes
+    held_count = reduced.shape[0]
     me = lax.axis_index("dp")
     rank = lax.axis_index("mp")
     chips = groups // 2
@@ -467,7 +469,8 @@
         infos.append(copy)
     moves = []
     locals_ = []
-    for c in range(chunks):
+
+    def dispatch(c):
         moves.append([])
         for d in range(1, groups):
             peer = (me + d) % groups
@@ -487,6 +490,8 @@
         )
         copy.start()
         locals_.append(copy)
+
+    dispatch(0)
 
     info_land[me] = info[me]
     for copy in infos:
@@ -514,6 +519,11 @@
     )
     loads[2].wait()
     shifted[...] = jnp.dot(place[...], res[...], preferred_element_type=jnp.float32)
+
+    new = lax.broadcasted_iota(jnp.int32, (mixed, mixed), 0)
+    old = lax.broadcasted_iota(jnp.int32, (mixed, mixed), 1)
+    old_at = new % block * groups + new // block % chips * 2 + new // (block * chips)
+    turn[...] = jnp.where(old == old_at, 1.0, 0.0).astype(jnp.bfloat16)
 
     scale = math.log2(math.e) / math.sqrt(HD)
     tall = stack * rows
@@ -741,6 +751,8 @@
         for copy in moves[c]:
             copy.wait_recv()
         locals_[c].wait()
+        if c + 1 < chunks:
+            dispatch(c + 1)
         if c == 0:
             loads[0].wait()
             loads[1].wait()
@@ -807,46 +819,54 @@
 
     direct_rows = upright(direct)
     norm_rows = upright(norm)
-    nears = []
     for c in range(chunks):
         here = pl.ds(c * mixed, mixed)
-        upstream[here, :] = (
+        part = (
             direct_rows[c * mixed : (c + 1) * mixed] * scaled_head
             - norm_rows[c * mixed : (c + 1) * mixed] * combined[here, :]
         ).astype(jnp.bfloat16)
-        slopes = lax.dot_general(
-            upstream[here, :], w[...], NT, preferred_element_type=jnp.float32
-        ).reshape(block, groups, width)
-        there = pl.ds(c * block, block)
-        for g in range(groups):
-            full_parts[g % 2, g // 2, there, :] = slopes[:, g, :]
-            half_parts[g % 2, g // 2, there, :] = slopes[:, g, :].astype(jnp.bfloat16)
-        copy = remote(
-            half_parts.at[1 - core, :, there, :],
-            near_land.at[:, there, :],
-            near_sem,
-            (c,),
-            dp=sibling,
-        )
+        upstream[here, :] = part
+        part = jnp.dot(turn[...], part, preferred_element_type=jnp.float32).astype(jnp.bfloat16)
+        for k in range(groups):
+            turned[k // chips, pl.ds(k % chips * held_count + c * block, block), :] = part[
+                k * block : (k + 1) * block
+            ]
+    halves = near_send.shape[0]
+    half = width // halves
+    nears = []
+    for k in range(halves):
+        near_send[k] = lax.dot_general(
+            turned[1 - core],
+            w[k * half : (k + 1) * half, :],
+            NT,
+            preferred_element_type=jnp.float32,
+        ).astype(jnp.bfloat16)
+        copy = remote(near_send.at[k], near_land.at[k], near_sem, (k,), dp=sibling)
         copy.start()
         nears.append(copy)
-
     fars = []
-    for c in range(chunks):
-        there = pl.ds(c * block, block)
-        nears[c].wait_recv()
+    for k in range(halves):
+        slopes = own.at[pl.ds(0, chips * held_count), pl.ds(0, half)]
+        slopes[...] = lax.dot_general(
+            turned[core],
+            w[k * half : (k + 1) * half, :],
+            NT,
+            preferred_element_type=jnp.float32,
+        )
+        nears[k].wait_recv()
         for q in range(chips):
             goal = (chip + q) % chips
-            both = full_parts[core, goal, there, :] + near_land[goal, there, :].astype(jnp.float32)
+            there = at(goal * held_count, held_count)
+            both = slopes[there, :] + near_land[k, there, :].astype(jnp.float32)
             if q == 0:
-                reduced[there, :] = both
+                reduced[:, k * half : (k + 1) * half] = both
             else:
-                far_send[q - 1, there, :] = both.astype(jnp.bfloat16)
+                far_send[k, q - 1] = both.astype(jnp.bfloat16)
                 copy = remote(
-                    far_send.at[q - 1, there, :],
-                    far_land.at[q - 1, there, :],
+                    far_send.at[k, q - 1],
+                    far_land.at[k, q - 1],
                     far_sem,
-                    (c * (chips - 1) + q - 1,),
+                    (k * (chips - 1) + q - 1,),
                     dp=goal * 2 + core,
                 )
                 copy.start()
@@ -861,14 +881,13 @@
     loss_out[...] = jnp.sum(soft, axis=0, keepdims=True) / pairs
     head_gradient[...] = jnp.sum(direct_rows * combined[...], axis=0, keepdims=True) * gain[...]
 
-    for c in range(chunks):
-        there = pl.ds(c * block, block)
+    for k in range(halves):
         extra = None
         for q in range(1, chips):
-            fars[c * (chips - 1) + q - 1].wait_recv()
-            piece = far_land[q - 1, there, :].astype(jnp.float32)
+            fars[k * (chips - 1) + q - 1].wait_recv()
+            piece = far_land[k, q - 1].astype(jnp.float32)
             extra = piece if extra is None else extra + piece
-        reduced[there, :] += extra
+        reduced[:, k * half : (k + 1) * half] += extra
 
     for copy in backs:
         copy.wait_recv()
@@ -941,7 +960,7 @@
     bf16, f32 = jnp.bfloat16, jnp.float32
     vmem = pl.BlockSpec(memory_space=pltpu.VMEM)
     smem = pl.BlockSpec(memory_space=pltpu.SMEM)
-    hbm = pl.BlockSpec(memory_space=pl.ANY)
+    hbm = pl.BlockSpec(memory_space=pltpu.HBM)
     packed, info, target = pl.pallas_call(
         functools.partial(plan_kernel, per, chunk_slots, window),
         out_shape=(
@@ -963,6 +982,8 @@
     slots = held_count * slot_count
     sub = SUB
     steps = count // sub
+    halves = 2
+    half = width // halves
     dma = lambda *shape: pltpu.SemaphoreType.DMA(shape)
     returned, pooled, upstream, reduced, head_gradient, rewards, loss = pl.pallas_call(
         functools.partial(
@@ -987,6 +1008,7 @@
             pltpu.VMEM((count, columns), bf16),
             pltpu.VMEM((count, count), bf16),
             pltpu.VMEM((count // 2, count), f32),
+            pltpu.VMEM((groups * block, groups * block), bf16),
             pltpu.VMEM((count, columns), f32),
             pltpu.VMEM((slots, width), bf16),
             pltpu.VMEM((count, columns), f32),
@@ -996,11 +1018,11 @@
             pltpu.VMEM((count, columns), f32),
             pltpu.VMEM((8, HD), f32),
             pltpu.VMEM((groups, 8, HD), f32),
-            pltpu.VMEM((2, chips, held_count, width), f32),
-            pltpu.VMEM((2, chips, held_count, width), bf16),
-            pltpu.VMEM((chips, held_count, width), bf16),
-            pltpu.VMEM((chips - 1, held_count, width), bf16),
-            pltpu.VMEM((chips - 1, held_count, width), bf16),
+            pltpu.VMEM((2, chips * held_count, columns), bf16),
+            pltpu.VMEM((halves, chips * held_count, half), bf16),
+            pltpu.VMEM((halves, chips * held_count, half), bf16),
+            pltpu.VMEM((halves, chips - 1, held_count, half), bf16),
+            pltpu.VMEM((halves, chips - 1, held_count, half), bf16),
             dma(4),
             dma(2, groups - 1),
             dma(2, chunks * (groups - 1)),
@@ -1011,8 +1033,8 @@
             dma(2, 2, steps),
             dma(2, steps),
             dma(2, groups - 1),
-            dma(2, chunks),
-            dma(2, chunks * (chips - 1)),
+            dma(2, halves),
+            dma(2, halves * (chips - 1)),
         ],
         compiler_params=pltpu.CompilerParams(
             collective_id=0, has_side_effects=True, vmem_limit_bytes=44 << 20
@@ -1070,7 +1092,7 @@
     )
 
 
-SUB = 64
+SUB = 32
 
 
 def kv_window(planes, local_heads):

time: 99.2 us -> 93.1 us (0.939)
  Pallas kernels: 89.5 us -> 83.4 us
    pallas_call x1, Pallas kernels: 79.9 us -> 73.8 us  [fused_shards(): pl.pallas_call(functools.partial(layer_kernel, (groups, planes, per, chun...]
where the time goes in v2:
time: 93.1 us; the launch traced here: 92.8 us
  Pallas kernels  83.4 us (90%)
  local copies, waits for them, and re-layouts  6.34 us (7%)
  between operations  2.49 us (3%)
    pallas_call x1, Pallas kernels, fused_shards(): pl.pallas_call(functools.partial(layer_kernel, (groups, planes, per, chun...  73.8 us
    pallas_call x1, Pallas kernels, fused_shards(): pl.pallas_call(functools.partial(gradient_kernel, per, chunk_slots), out_...  6.95 us
    unnamed x21, local copies, waits for them, and re-layouts  6.34 us
    pallas_call x1, Pallas kernels, fused_shards(): pl.pallas_call(functools.partial(plan_kernel, per, chunk_slots, window),...  2.65 us

profile of v2, /device:TPU:0, one launch (start us, length us, event | category | flops | bytes accessed | tf_op | source)
XLA Modules:
  0.0 92.8 jit_solution(14390510182275940880)
XLA Ops:
  0.6 0.0 copy-start.1
  0.6 1.3 %copy-done.1 = bf16[48,8,1536]{2,1,0:T(8,128)(2,1)S(1)} copy-done((bf16[48,8,1536]{2,1,0:T(8,128)(2,1)S(1)}, bf16[48,8,1536]{2,1,0:T(8,128)(2,1)}, u32[]{:S(2)}) %copy-start.1) | copy-done | bytes 1179672
  1.9 0.0 copy-start.2
  1.9 1.3 %copy-done.2 = bf16[2,48,8,768]{3,2,1,0:T(8,128)(2,1)S(1)} copy-done((bf16[2,48,8,768]{3,2,1,0:T(8,128)(2,1)S(1)}, bf16[2,48,8,768]{3,2,1,0:T(8,128)(2,1)}, u32[]{:S(2)}) %copy-start.2) | copy-done | bytes 1179672
  3.2 0.0 copy-start.6
  3.2 0.7 copy-done.6
  3.8 0.0 copy-start.8
  3.8 0.7 copy-done.8
  4.5 0.0 copy-start.3
  4.5 0.0 copy-start.4
  4.5 0.0 copy-start.5
  4.5 2.6 %plan.1 = (bf16[48,8,2048]{2,1,0:T(8,128)(2,1)S(1)}, f32[8,16,128]{2,1,0:T(8,128)S(1)}, s32[48]{0:T(128)S(1)}) custom-call(s32[48]{0:T(128)S(1)} %copy-done.8, s32[48]{0:T(128)S(1)} %copy-done.6, bf16[48,8,1536]{2,1,0:T(8,128)(2,1)S(1)} %copy-done.1, bf16[2,48,8,768]{3,2,1,0:T(8,128)(2,1)S(1)} %copy-done.2), custom_call_target="tpu_custom_call" | custom-call | tf_op jit(solution)/shard_map/plan/pallas_call | solution.py:964
  7.2 0.0 copy-done.9
  7.2 0.0 copy-done.3
  7.2 0.0 copy-done.4
  7.2 0.0 copy-done.5
  7.2 0.0 copy-start
  7.2 1.9 %copy-done = bf16[2,1,1024,768]{3,2,1,0:T(8,128)(2,1)S(1)} copy-done((bf16[2,1,1024,768]{3,2,1,0:T(8,128)(2,1)S(1)}, bf16[2,1,1024,768]{3,2,1,0:T(8,128)(2,1)}, u32[]{:S(2)}) %copy-start) | copy-done | bytes 3145752
  9.1 0.0 copy-start.7
  9.1 73.8 %layer.1 = (bf16[384,1536]{1,0:T(8,128)(2,1)S(1)}, bf16[384,1536]{1,0:T(8,128)(2,1)S(1)}, bf16[384,1024]{1,0:T(8,128)(2,1)S(1)}, f32[48,1536]{1,0:T(8,128)S(1)},...) custom-call(bf16[384,2048]{1,0:T(8,128)(2,1)S(1)} %bitcast.6, ...), custom_call_target="tpu_custom_call" | custom-call | tf_op jit(solution)/shard_map/layer/pallas_call | solution.py:988
  82.9 0.0 copy-done.7
  82.9 6.9 %gradient.1 = (bf16[48,8,1536]{2,1,0:T(8,128)(2,1)}, f32[48,1536]{1,0:T(8,128)}, f32[1536,1024]{1,0:T(8,128)}) custom-call(s32[48]{0:T(128)S(1)} %get-tuple-element.19.target, s32[48]{0:T(128)S(1)} %copy-done.7, bf16[48,8,1536]{2,1,0:T(8,128)(2,1)S(1)} %bitcast.7, f32[48,1536]{1,0:T(8,128)S(1)} %get-tuple-element.23.reduced, ...), custom_call_target="tpu_custom_call" | custom-call | tf_op jit(solution)/shard_map/gradient/pallas_call | solution.py:1054
  89.9 0.6 reduce
  91.1 0.6 copy.19
  (2 shorter events, 0.0 us)
Async XLA Ops:
  0.6 1.3 %copy-start.1 = (bf16[48,8,1536]{2,1,0:T(8,128)(2,1)S(1)}, bf16[48,8,1536]{2,1,0:T(8,128)(2,1)}, u32[]{:S(2)}) copy-start(bf16[48,8,1536]{2,1,0:T(8,128)(2,1)} %query.1) | copy-start | bytes 3538948
  1.9 1.3 %copy-start.2 = (bf16[2,48,8,768]{3,2,1,0:T(8,128)(2,1)S(1)}, bf16[2,48,8,768]{3,2,1,0:T(8,128)(2,1)}, u32[]{:S(2)}) copy-start(bf16[2,48,8,768]{3,2,1,0:T(8,128)(2,1)} %keys.1) | copy-start | bytes 3538948
  3.2 0.7 copy-start.6
  3.8 0.7 copy-start.8
  4.5 2.7 %copy-start.9 = (s32[384]{0:T(512)S(1)}, s32[384]{0:T(512)}, u32[]{:S(2)}) copy-start(s32[384]{0:T(512)} %param.15) | copy-start | bytes 4612
  4.5 2.7 %copy-start.3 = (bf16[384,1024]{1,0:T(8,128)(2,1)S(1)}, bf16[384,1024]{1,0:T(8,128)(2,1)}, u32[]{:S(2)}) copy-start(bf16[384,1024]{1,0:T(8,128)(2,1)} %residual.1) | copy-start | bytes 2359300
  4.5 2.7 %copy-start.4 = (f32[1024]{0:T(1024)S(1)}, f32[1024]{0:T(1024)}, u32[]{:S(2)}) copy-start(f32[1024]{0:T(1024)} %param.18) | copy-start | bytes 12292
  4.5 2.7 %copy-start.5 = (f32[1024]{0:T(1024)S(1)}, f32[1024]{0:T(1024)}, u32[]{:S(2)}) copy-start(f32[1024]{0:T(1024)} %param.19) | copy-start | bytes 12292
  7.2 1.9 %copy-start = (bf16[2,1,1024,768]{3,2,1,0:T(8,128)(2,1)S(1)}, bf16[2,1,1024,768]{3,2,1,0:T(8,128)(2,1)}, u32[]{:S(2)}) copy-start(bf16[2,1,1024,768]{3,2,1,0:T(8,128)(2,1)} %cache.1) | copy-start | bytes 9437188
  9.1 73.8 %copy-start.7 = (s32[48]{0:T(128)S(1)}, s32[48]{0:T(128)}, u32[]{:S(2)}) copy-start(s32[48]{0:T(128)} %lengths.3) | copy-start | bytes 580

commit v3 on v2

--- a/solution.py
+++ b/solution.py
@@ -758,12 +758,13 @@
             loads[1].wait()
         attend(c)
         share(c)
+        if c == chunks - 1:
+            for n in range((chunks - 2) * steps):
+                inner(n)
         if c > 0:
             pass_on(c - 1)
             mix(c - 1)
     taken = (chunks - 2) * steps
-    for n in range(taken):
-        inner(n)
     pass_on(chunks - 1)
     for c in range(chunks):
         give_back(c)
@@ -976,7 +977,7 @@
             pltpu.VMEM((2, held_count, slot_count, span), bf16),
             pltpu.SemaphoreType.DMA((3,)),
         ],
-        compiler_params=pltpu.CompilerParams(vmem_limit_bytes=16 << 20),
+        compiler_params=pltpu.CompilerParams(vmem_limit_bytes=61 << 20),
         name="plan",
     )(owners, lengths, response_query, response_keys)
     slots = held_count * slot_count
@@ -1050,7 +1051,7 @@
         reward_head[None],
         pairing[None],
     )
-    tile = 256
+    tile = 512
     attention_rows, pooled_gradient, weight_gradient = pl.pallas_call(
         functools.partial(gradient_kernel, per, chunk_slots),
         out_shape=(

time: 93.1 us -> 91.4 us (0.982)
  local copies, waits for them, and re-layouts: 6.34 us -> 4.75 us
    unnamed x21 -> x19, local copies, waits for them, and re-layouts: 6.34 us -> 4.75 us
    pallas_call x1, Pallas kernels: 2.65 us -> 3.65 us  [fused_shards(): pl.pallas_call(functools.partial(plan_kernel, per, chunk_slots, window),...]
    pallas_call x1, Pallas kernels: 6.95 us -> 6.01 us  [fused_shards(): pl.pallas_call(functools.partial(gradient_kernel, per, chunk_slots), out_...]
where the time goes in v3:
time: 91.4 us; the launch traced here: 91.1 us
  Pallas kernels  83.2 us (91%)
  local copies, waits for them, and re-layouts  4.75 us (5%)
  between operations  2.51 us (3%)
    pallas_call x1, Pallas kernels, fused_shards(): pl.pallas_call(functools.partial(layer_kernel, (groups, planes, per, chun...  73.6 us
    pallas_call x1, Pallas kernels, fused_shards(): pl.pallas_call(functools.partial(gradient_kernel, per, chunk_slots), out_...  6.01 us
    unnamed x19, local copies, waits for them, and re-layouts  4.75 us
    pallas_call x1, Pallas kernels, fused_shards(): pl.pallas_call(functools.partial(plan_kernel, per, chunk_slots, window),...  3.65 us

profile of v3, /device:TPU:0, one launch (start us, length us, event | category | flops | bytes accessed | tf_op | source)
XLA Modules:
  0.0 91.1 jit_solution(8482685373709212788)
XLA Ops:
  0.6 0.0 copy-start.8
  0.6 0.0 copy-start.4
  0.7 0.0 copy-start.5
  0.7 0.0 copy-start.2
  0.7 3.6 %plan.1 = (bf16[48,8,2048]{2,1,0:T(8,128)(2,1)}, f32[8,16,128]{2,1,0:T(8,128)}, s32[48]{0:T(128)}) custom-call(s32[48]{0:T(128)} %owners.1, s32[48]{0:T(128)} %lengths.3, bf16[48,8,1536]{2,1,0:T(8,128)(2,1)} %query.1, bf16[2,48,8,768]{3,2,1,0:T(8,128)(2,1)} %keys.1), custom_call_target="tpu_custom_call" | custom-call | tf_op jit(solution)/shard_map/plan/pallas_call | solution.py:965
  4.3 0.0 copy-done.8
  4.4 0.0 copy-done.4
  4.4 0.0 copy-done.5
  4.4 0.0 copy-done.2
  4.4 0.0 copy-start
  4.4 1.9 %copy-done = bf16[2,1,1024,768]{3,2,1,0:T(8,128)(2,1)S(1)} copy-done((bf16[2,1,1024,768]{3,2,1,0:T(8,128)(2,1)S(1)}, bf16[2,1,1024,768]{3,2,1,0:T(8,128)(2,1)}, u32[]{:S(2)}) %copy-start) | copy-done | bytes 3145752
  6.3 0.0 copy-start.1
  6.3 1.4 %copy-done.1 = bf16[48,8,2048]{2,1,0:T(8,128)(2,1)S(1)} copy-done((bf16[48,8,2048]{2,1,0:T(8,128)(2,1)S(1)}, bf16[48,8,2048]{2,1,0:T(8,128)(2,1)}, u32[]{:S(2)}) %copy-start.1) | copy-done | bytes 1572888
  7.7 0.0 copy-start.3
  7.7 0.8 copy-done.3
  8.5 0.0 copy-start.6
  8.5 0.0 copy-start.7
  8.5 73.6 %layer.1 = (bf16[384,1536]{1,0:T(8,128)(2,1)S(1)}, bf16[384,1536]{1,0:T(8,128)(2,1)S(1)}, bf16[384,1024]{1,0:T(8,128)(2,1)S(1)}, f32[48,1536]{1,0:T(8,128)S(1)},...) custom-call(bf16[384,2048]{1,0:T(8,128)(2,1)S(1)} %bitcast.6, f32[8,16,128]{2,1,0:T(8,128)S(1)} %copy-done.3, ...), custom_call_target="tpu_custom_call" | custom-call | tf_op jit(solution)/shard_map/layer/pallas_call | solution.py:989
  82.1 0.0 copy-done.6
  82.1 0.0 copy-done.7
  82.1 6.0 %gradient.1 = (bf16[48,8,1536]{2,1,0:T(8,128)(2,1)}, f32[48,1536]{1,0:T(8,128)}, f32[1536,1024]{1,0:T(8,128)}) custom-call(s32[48]{0:T(128)S(1)} %copy-done.7, s32[48]{0:T(128)S(1)} %copy-done.6, bf16[48,8,1536]{2,1,0:T(8,128)(2,1)S(1)} %bitcast.7, f32[48,1536]{1,0:T(8,128)S(1)} %get-tuple-element.23.reduced, ...), custom_call_target="tpu_custom_call" | custom-call | tf_op jit(solution)/shard_map/gradient/pallas_call | solution.py:1055
  88.1 0.6 reduce
  89.4 0.6 copy.19
  (1 shorter events, 0.0 us)
Async XLA Ops:
  0.6 3.7 %copy-start.8 = (s32[384]{0:T(512)S(1)}, s32[384]{0:T(512)}, u32[]{:S(2)}) copy-start(s32[384]{0:T(512)} %param.15) | copy-start | bytes 4612
  0.6 3.7 %copy-start.4 = (f32[1024]{0:T(1024)S(1)}, f32[1024]{0:T(1024)}, u32[]{:S(2)}) copy-start(f32[1024]{0:T(1024)} %param.18) | copy-start | bytes 12292
  0.7 3.7 %copy-start.5 = (f32[1024]{0:T(1024)S(1)}, f32[1024]{0:T(1024)}, u32[]{:S(2)}) copy-start(f32[1024]{0:T(1024)} %param.19) | copy-start | bytes 12292
  0.7 3.7 %copy-start.2 = (bf16[384,1024]{1,0:T(8,128)(2,1)S(1)}, bf16[384,1024]{1,0:T(8,128)(2,1)}, u32[]{:S(2)}) copy-start(bf16[384,1024]{1,0:T(8,128)(2,1)} %residual.1) | copy-start | bytes 2359300
  4.4 1.9 %copy-start = (bf16[2,1,1024,768]{3,2,1,0:T(8,128)(2,1)S(1)}, bf16[2,1,1024,768]{3,2,1,0:T(8,128)(2,1)}, u32[]{:S(2)}) copy-start(bf16[2,1,1024,768]{3,2,1,0:T(8,128)(2,1)} %cache.1) | copy-start | bytes 9437188
  6.3 1.4 %copy-start.1 = (bf16[48,8,2048]{2,1,0:T(8,128)(2,1)S(1)}, bf16[48,8,2048]{2,1,0:T(8,128)(2,1)}, u32[]{:S(2)}) copy-start(bf16[48,8,2048]{2,1,0:T(8,128)(2,1)} %get-tuple-element.20) | copy-start | bytes 4718596
  7.7 0.8 copy-start.3
  8.5 73.6 %copy-start.6 = (s32[48]{0:T(128)S(1)}, s32[48]{0:T(128)}, u32[]{:S(2)}) copy-start(s32[48]{0:T(128)} %lengths.3) | copy-start | bytes 580
  8.5 73.6 %copy-start.7 = (s32[48]{0:T(128)S(1)}, s32[48]{0:T(128)}, u32[]{:S(2)}) copy-start(s32[48]{0:T(128)} %get-tuple-element.19.target) | copy-start | bytes 580

commit v4 on v3

--- a/solution.py
+++ b/solution.py
@@ -525,6 +525,10 @@
     old_at = new % block * groups + new // block % chips * 2 + new // (block * chips)
     turn[...] = jnp.where(old == old_at, 1.0, 0.0).astype(jnp.bfloat16)
 
+    for copy in moves[0]:
+        copy.wait_send()
+    if chunks > 1:
+        dispatch(1)
     scale = math.log2(math.e) / math.sqrt(HD)
     tall = stack * rows
 
@@ -751,7 +755,7 @@
         for copy in moves[c]:
             copy.wait_recv()
         locals_[c].wait()
-        if c + 1 < chunks:
+        if 0 < c < chunks - 1:
             dispatch(c + 1)
         if c == 0:
             loads[0].wait()
@@ -895,7 +899,7 @@
     for copy in locals_[chunks:]:
         copy.wait()
     sent = infos + backs + stats + nears + fars
-    for group in moves + pools + passes:
+    for group in moves[1:] + pools + passes:
         sent = sent + group
     for copy in sent + z_copies:
         copy.wait_send()

time: 91.4 us -> 90.1 us (0.986)
  Pallas kernels: 83.2 us -> 82 us
    pallas_call x1, Pallas kernels: 73.6 us -> 72.3 us  [fused_shards(): pl.pallas_call(functools.partial(layer_kernel, (groups, planes, per, chun...]
where the time goes in v4:
time: 90.1 us; the launch traced here: 89.8 us
  Pallas kernels  82 us (91%)
  local copies, waits for them, and re-layouts  4.75 us (5%)
  between operations  2.51 us (3%)
    pallas_call x1, Pallas kernels, fused_shards(): pl.pallas_call(functools.partial(layer_kernel, (groups, planes, per, chun...  72.3 us
    pallas_call x1, Pallas kernels, fused_shards(): pl.pallas_call(functools.partial(gradient_kernel, per, chunk_slots), out_...  6.01 us
    unnamed x19, local copies, waits for them, and re-layouts  4.75 us
    pallas_call x1, Pallas kernels, fused_shards(): pl.pallas_call(functools.partial(plan_kernel, per, chunk_slots, window),...  3.65 us

profile of v4, /device:TPU:0, one launch (start us, length us, event | category | flops | bytes accessed | tf_op | source)
XLA Modules:
  0.0 89.8 jit_solution(13643695673126410709)
XLA Ops:
  0.6 0.0 copy-start.8
  0.6 0.0 copy-start.4
  0.7 0.0 copy-start.5
  0.7 0.0 copy-start.2
  0.7 3.6 %plan.1 = (bf16[48,8,2048]{2,1,0:T(8,128)(2,1)}, f32[8,16,128]{2,1,0:T(8,128)}, s32[48]{0:T(128)}) custom-call(s32[48]{0:T(128)} %owners.1, s32[48]{0:T(128)} %lengths.3, bf16[48,8,1536]{2,1,0:T(8,128)(2,1)} %query.1, bf16[2,48,8,768]{3,2,1,0:T(8,128)(2,1)} %keys.1), custom_call_target="tpu_custom_call" | custom-call | tf_op jit(solution)/shard_map/plan/pallas_call | solution.py:969
  4.3 0.0 copy-done.8
  4.4 0.0 copy-done.4
  4.4 0.0 copy-done.5
  4.4 0.0 copy-done.2
  4.4 0.0 copy-start
  4.4 1.9 %copy-done = bf16[2,1,1024,768]{3,2,1,0:T(8,128)(2,1)S(1)} copy-done((bf16[2,1,1024,768]{3,2,1,0:T(8,128)(2,1)S(1)}, bf16[2,1,1024,768]{3,2,1,0:T(8,128)(2,1)}, u32[]{:S(2)}) %copy-start) | copy-done | bytes 3145752
  6.3 0.0 copy-start.1
  6.3 1.4 %copy-done.1 = bf16[48,8,2048]{2,1,0:T(8,128)(2,1)S(1)} copy-done((bf16[48,8,2048]{2,1,0:T(8,128)(2,1)S(1)}, bf16[48,8,2048]{2,1,0:T(8,128)(2,1)}, u32[]{:S(2)}) %copy-start.1) | copy-done | bytes 1572888
  7.7 0.0 copy-start.3
  7.7 0.8 copy-done.3
  8.5 0.0 copy-start.6
  8.5 0.0 copy-start.7
  8.5 72.3 %layer.1 = (bf16[384,1536]{1,0:T(8,128)(2,1)S(1)}, bf16[384,1536]{1,0:T(8,128)(2,1)S(1)}, bf16[384,1024]{1,0:T(8,128)(2,1)S(1)}, f32[48,1536]{1,0:T(8,128)S(1)},...) custom-call(bf16[384,2048]{1,0:T(8,128)(2,1)S(1)} %bitcast.6, f32[8,16,128]{2,1,0:T(8,128)S(1)} %copy-done.3, ...), custom_call_target="tpu_custom_call" | custom-call | tf_op jit(solution)/shard_map/layer/pallas_call | solution.py:993
  80.8 0.0 copy-done.6
  80.9 0.0 copy-done.7
  80.9 6.0 %gradient.1 = (bf16[48,8,1536]{2,1,0:T(8,128)(2,1)}, f32[48,1536]{1,0:T(8,128)}, f32[1536,1024]{1,0:T(8,128)}) custom-call(s32[48]{0:T(128)S(1)} %copy-done.7, s32[48]{0:T(128)S(1)} %copy-done.6, bf16[48,8,1536]{2,1,0:T(8,128)(2,1)S(1)} %bitcast.7, f32[48,1536]{1,0:T(8,128)S(1)} %get-tuple-element.23.reduced, ...), custom_call_target="tpu_custom_call" | custom-call | tf_op jit(solution)/shard_map/gradient/pallas_call | solution.py:1059
  86.9 0.6 reduce
  88.1 0.6 copy.19
  (1 shorter events, 0.0 us)
Async XLA Ops:
  0.6 3.7 %copy-start.8 = (s32[384]{0:T(512)S(1)}, s32[384]{0:T(512)}, u32[]{:S(2)}) copy-start(s32[384]{0:T(512)} %param.15) | copy-start | bytes 4612
  0.6 3.7 %copy-start.4 = (f32[1024]{0:T(1024)S(1)}, f32[1024]{0:T(1024)}, u32[]{:S(2)}) copy-start(f32[1024]{0:T(1024)} %param.18) | copy-start | bytes 12292
  0.7 3.7 %copy-start.5 = (f32[1024]{0:T(1024)S(1)}, f32[1024]{0:T(1024)}, u32[]{:S(2)}) copy-start(f32[1024]{0:T(1024)} %param.19) | copy-start | bytes 12292
  0.7 3.7 %copy-start.2 = (bf16[384,1024]{1,0:T(8,128)(2,1)S(1)}, bf16[384,1024]{1,0:T(8,128)(2,1)}, u32[]{:S(2)}) copy-start(bf16[384,1024]{1,0:T(8,128)(2,1)} %residual.1) | copy-start | bytes 2359300
  4.4 1.9 %copy-start = (bf16[2,1,1024,768]{3,2,1,0:T(8,128)(2,1)S(1)}, bf16[2,1,1024,768]{3,2,1,0:T(8,128)(2,1)}, u32[]{:S(2)}) copy-start(bf16[2,1,1024,768]{3,2,1,0:T(8,128)(2,1)} %cache.1) | copy-start | bytes 9437188
  6.3 1.4 %copy-start.1 = (bf16[48,8,2048]{2,1,0:T(8,128)(2,1)S(1)}, bf16[48,8,2048]{2,1,0:T(8,128)(2,1)}, u32[]{:S(2)}) copy-start(bf16[48,8,2048]{2,1,0:T(8,128)(2,1)} %get-tuple-element.20) | copy-start | bytes 4718596
  7.7 0.8 copy-start.3
  8.5 72.3 %copy-start.6 = (s32[48]{0:T(128)S(1)}, s32[48]{0:T(128)}, u32[]{:S(2)}) copy-start(s32[48]{0:T(128)} %lengths.3) | copy-start | bytes 580
  8.5 72.3 %copy-start.7 = (s32[48]{0:T(128)S(1)}, s32[48]{0:T(128)}, u32[]{:S(2)}) copy-start(s32[48]{0:T(128)} %get-tuple-element.19.target) | copy-start | bytes 580
